TPU v7x, 32 devices: a whole 2x2x4 slice. The times are simulated.
32 devices in a mesh: layer: 4 (over y, x), row: 8 (over z, core).
Axes of the slice: x: 2, y: 2, z: 4, core: 2. Of those that a mesh axis runs over, the one named last changes fastest.
Arguments:
- tokens: bfloat16 [16, 8192], P('row'), may hold values from -6 to 6
- up_weight: bfloat16 [4, 32768, 8192], P('layer', 'row'), may hold values from -6 to 6
- hess_panel: float32 [4, 256, 8192], P('layer', None, 'row'), may hold values from -1 to 2, as said below
- keep_mask: int32 [4, 32768, 256], P('layer', 'row'), may hold values from 0 to 1, as said below
Outputs:
- section_acts: bfloat16 [4, 16, 8192], P('layer', 'row')
- pruned_blocks: bfloat16 [4, 32768, 256], P('layer', 'row')
Inputs may be any that keep to these rules, and one draw needn't show every extreme that they name: `keep_mask`: each row has exactly 64 ones in each block of 128 columns. `hess_panel`: zero where the column is below the row; the diagonal lies in [0.5, 2].
All inputs are finite; a program needn't handle non-finite values.
Results may differ from a plain program's by a relative error of at most 0.017.
Values may be sent and summed in bfloat16 or wider, within the bound.
No kernel may reach another device: no remote copies, remote signals or barrier semaphores. Data moves between devices by JAX's collectives and lax.ppermute only.
A program may use at most 384 MiB of HBM per device.

v0:
```python
import jax
import jax.numpy as jnp
from jax import lax
from jax.sharding import PartitionSpec as P

BLOCK = 128


epsilon = 1e-05


def passed_along(array, axis, by):
    size = lax.axis_size(axis)
    pairs = [(i, i + by) for i in range(size) if 0 <= i + by < size]
    return lax.ppermute(array, axis, pairs)


def highest_dot(left, right):
    return jnp.dot(left, right, precision=lax.Precision.HIGHEST, preferred_element_type=jnp.float32)


def eliminate(columns_in, pivot_block, retained):
    count = pivot_block.shape[0]
    width_sub = min(16, count)
    inverse = 1.0 / jnp.diagonal(pivot_block)
    dropped = 1.0 - retained.astype(jnp.float32)
    residual = columns_in
    error_list = []
    for start in range(0, count, width_sub):
        finish = start + width_sub
        current = residual[:, start:finish]
        local_errors = []
        for offset in range(width_sub):
            index_col = start + offset
            error = (
                current[:, offset : offset + 1]
                * dropped[:, index_col : index_col + 1]
                * inverse[index_col]
            )
            current = current - error * pivot_block[index_col : index_col + 1, start:finish]
            local_errors.append(error)
        sub_errors = jnp.concatenate(local_errors, 1)
        error_list.append(sub_errors)
        pieces = [residual[:, :start], current]
        if finish < count:
            pieces.append(
                residual[:, finish:] - highest_dot(sub_errors, pivot_block[start:finish, finish:])
            )
        residual = jnp.concatenate(pieces, 1)
    return (residual, jnp.concatenate(error_list, 1))


def prune_layer(weight, panel, retained):
    width_block = panel.shape[0] // 2
    leading = weight[:, : 2 * width_block].astype(jnp.float32)
    first_values, errors_first = eliminate(
        leading[:, :width_block], panel[:width_block, :width_block], retained[:, :width_block]
    )
    second_in = leading[:, width_block:] - highest_dot(
        errors_first, panel[:width_block, width_block : 2 * width_block]
    )
    second_values, errors_second = eliminate(
        second_in, panel[width_block:, width_block : 2 * width_block], retained[:, width_block:]
    )
    pruned = jnp.concatenate([first_values, second_values], 1).astype(jnp.bfloat16)
    return (pruned, jnp.concatenate([errors_first, errors_second], 1))


def transposed_dot(left, right):
    return lax.dot_general(
        left, right, (((1,), (1,)), ((), ())), preferred_element_type=jnp.float32
    )


def transposed_highest(left, right):
    return lax.dot_general(
        left,
        right,
        (((1,), (1,)), ((), ())),
        precision=lax.Precision.HIGHEST,
        preferred_element_type=jnp.float32,
    )


def per_device(tokens, up_weight, hess_panel, keep_mask):
    weight = up_weight[0]
    local_panel = hess_panel[0]
    retained = keep_mask[0]
    leading_count = 2 * BLOCK
    features = weight.shape[1]
    full_panel = lax.all_gather(local_panel.astype(jnp.bfloat16), "row", axis=1, tiled=True).astype(
        local_panel.dtype
    )
    pruned, errors = prune_layer(weight, full_panel[:, :leading_count], retained)
    remote_panel = full_panel[:, leading_count:]
    mixed_weight = jnp.concatenate([pruned, weight[:, leading_count:]], 1)
    position = lax.axis_index("layer")
    depth = lax.axis_size("layer")
    section_input = tokens
    results = jnp.zeros_like(tokens)
    for turn in range(depth):
        portion = lax.all_gather(section_input, "row", axis=0, tiled=True)
        product = transposed_dot(portion, mixed_weight)
        panel_inputs = transposed_highest(
            portion[:, leading_count:].astype(jnp.float32), remote_panel
        )
        correction = transposed_highest(panel_inputs, errors)
        layer_output = ((product - correction) * features ** (-0.5)).astype(jnp.bfloat16)
        spread = lax.all_to_all(layer_output, "row", split_axis=0, concat_axis=1, tiled=True)
        hidden = jax.nn.silu(spread.astype(jnp.float32))
        folded = hidden.reshape(section_input.shape[0], -1, features).sum(axis=1)
        combined = section_input.astype(jnp.float32) + folded
        moment = jnp.mean(combined * combined, axis=-1, keepdims=True)
        produced = (combined * lax.rsqrt(moment + epsilon)).astype(jnp.bfloat16)
        results = jnp.where(position == turn, produced, results)
        if turn + 1 < depth:
            section_input = passed_along(produced, "layer", 1)
    return (results[None], pruned[None])


def solution(mesh):
    in_specs = (
        P("row", None),
        P("layer", "row", None),
        P("layer", None, "row"),
        P("layer", "row", None),
    )
    out_specs = (P("layer", "row", None), P("layer", "row", None))
    return jax.shard_map(
        per_device, mesh=mesh, in_specs=in_specs, out_specs=out_specs, check_vma=False
    )
```

profile of v0, /device:TPU:0, one launch (start us, length us, event | category | flops | bytes accessed | tf_op | source)
XLA Modules:
  0.0 1148.7 jit_solution(16725632295753040028)
XLA Ops:
  9.3 5.6 copy.17
  15.0 79.7 %copy.16 = bf16[1,4096,8192]{1,2,0:T(8,128)(2,1)} copy(bf16[1,4096,8192]{2,1,0:T(8,128)(2,1)} %param.5) | data formatting | bytes 134217728 | tf_op args[1]
  94.7 15.8 %all-gather.1 = bf16[8,2,8192]{2,1,0:T(2,128)(2,1)S(1)} all-gather(bf16[1,2,8192]{2,1,0:T(2,128)(2,1)S(1)} %bitcast.3424), channel_id=1, replica_groups=mesh['layer'=4,'row'=8] {'row'}, dimensions={0}, use_global_device_ids=true | all-gather | bytes 294912 | tf_op jit(solution)/shard_map/all_gather | solution.py:102
  111.3 4.7 fusion.17
  116.1 4.1 slice_convert_fusion.2
  120.2 3.2 bitcast_convert_fusion
  123.4 3.3 copy-done.16
  203.1 2.5 convolution_subtract_fusion.2
  237.0 2.3 convolution_subtract_fusion.4
  361.3 2.2 fusion.194
  458.0 2.5 fusion.158
  464.7 20.3 %concatenate.111 = f32[4096,128]{0,1:T(8,128)} concatenate(f32[4096,1]{0,1:T(1,128)S(1)} %fusion.284, f32[4096,1]{0,1:T(1,128)S(1)} %fusion.283, f32[4096,1]{0,1:T(1,128)S(1)} %fusion.282, f32[4096,1]{0,1:T(1,128)S(1)} %fusion.281, f32[4096,1]{0,1:T(1,128)S(1)} %copy-done.115, f32[4096,1]{0,1:T(1,128)S(1)} %copy-done.157, f32[4096,1]{0,1:T(1,128)S(1)} %copy-done.189, ...), dimensions={1} | concatenate | bytes 4194304 | tf_op jit(solution)/shard_map/concatenate | solution.py:50
  485.0 3.5 convolution_subtract_fusion
  520.5 2.5 convolution_subtract_fusion.1
  553.4 2.3 convolution_subtract_fusion.3
  721.9 2.2 constant_dynamic-update-slice_fusion.14
  724.2 2.2 bitcast_dynamic-update-slice_fusion.13
  726.5 2.2 constant_dynamic-update-slice_fusion.13
  728.8 2.2 bitcast_dynamic-update-slice_fusion.12
  786.7 50.6 %concatenate.120 = f32[4096,256]{0,1:T(8,128)} concatenate(f32[4096,1]{0,1:T(1,128)S(1)} %fusion.284, f32[4096,1]{0,1:T(1,128)S(1)} %fusion.283, f32[4096,1]{0,1:T(1,128)S(1)} %copy-done.40, f32[4096,1]{0,1:T(1,128)S(1)} %copy-done.76, f32[4096,1]{0,1:T(1,128)S(1)} %copy-done.116, f32[4096,1]{0,1:T(1,128)} %copy-done.156, f32[4096,1]{0,1:T(1,128)} %copy-done.188, ...), dimensions={1} | concatenate | bytes 8388608 | tf_op jit(solution)/shard_map/concatenate | solution.py:66
  837.7 2.3 constant_dynamic-update-slice_fusion.6
  840.0 2.3 constant_dynamic-update-slice_fusion.5
  842.2 2.3 constant_dynamic-update-slice_fusion.4
  852.2 43.2 %slice_dynamic-update-slice_fusion = bf16[4096,8192]{0,1:T(8,128)(2,1)} fusion(bf16[4096,8192]{0,1:T(8,128)(2,1)} %constant_dynamic-update-slice_fusion, bf16[4096,8192]{0,1:T(8,128)(2,1)} %bitcast), kind=kLoop, calls=%fused_computation.2 | loop fusion | bytes 130023424 | tf_op jit(solution)/shard_map/concatenate | solution.py:96
  895.4 3.5 fusion.15
  898.9 2.9 fusion.313
  901.8 24.6 %fusion.8 = bf16[16,4096]{1,0:T(8,128)(2,1)} fusion(f32[16,4096]{1,0:T(8,128)} %fusion.313, bf16[16,8192]{1,0:T(8,128)(2,1)} %reshape.310, bf16[4096,8192]{0,1:T(8,128)(2,1)} %slice_dynamic-update-slice_fusion), kind=kOutput, calls=%fused_computation.30 | convolution fusion | flops 1073938432 | bytes 67764224 | tf_op jit(solution)/shard_map/dot_general | solution.py:70
  928.2 4.2 all-to-all-start
  934.7 4.6 all-to-all-done
  946.0 3.6 collective-permute-start
  951.9 15.3 %all-gather.2 = bf16[8,2,8192]{2,1,0:T(2,128)(2,1)} all-gather(bf16[1,2,8192]{2,1,0:T(2,128)(2,1)S(1)} %bitcast.3425), channel_id=1, replica_groups=mesh['layer'=4,'row'=8] {'row'}, dimensions={0}, use_global_device_ids=true | all-gather | bytes 294912 | tf_op jit(solution)/shard_map/all_gather | solution.py:102
  968.9 3.5 fusion.13
  972.5 2.8 fusion.314
  975.4 24.4 %fusion.5 = bf16[16,4096]{1,0:T(8,128)(2,1)} fusion(f32[16,4096]{1,0:T(8,128)} %fusion.314, bf16[16,8192]{1,0:T(8,128)(2,1)} %reshape.312, bf16[4096,8192]{0,1:T(8,128)(2,1)} %slice_dynamic-update-slice_fusion), kind=kOutput, calls=%fused_computation.27 | convolution fusion | flops 1073938432 | bytes 67764224 | tf_op jit(solution)/shard_map/dot_general | solution.py:70
  1001.6 4.4 all-to-all-start.1
  1008.2 4.6 all-to-all-done.1
  1019.5 3.5 collective-permute-start.1
  1025.0 14.2 %all-gather.3 = bf16[8,2,8192]{2,1,0:T(2,128)(2,1)S(1)} all-gather(bf16[1,2,8192]{2,1,0:T(2,128)(2,1)S(1)} %bitcast.3426), channel_id=1, replica_groups=mesh['layer'=4,'row'=8] {'row'}, dimensions={0}, use_global_device_ids=true | all-gather | bytes 294912 | tf_op jit(solution)/shard_map/all_gather | solution.py:102
  1039.3 3.4 fusion.11
  1045.0 22.8 %fusion.6 = bf16[16,4096]{1,0:T(8,128)(2,1)S(1)} fusion(f32[16,4096]{1,0:T(8,128)S(1)} %fusion.315, bf16[16,8192]{1,0:T(8,128)(2,1)S(1)} %reshape.314, bf16[4096,8192]{0,1:T(8,128)(2,1)} %slice_dynamic-update-slice_fusion), kind=kOutput, calls=%fused_computation.28 | convolution fusion | flops 1073938432 | bytes 67764224 | tf_op jit(solution)/shard_map/dot_general | solution.py:70
  1068.8 3.4 all-to-all-start.2
  1074.1 4.8 all-to-all-done.2
  1079.9 4.4 collective-permute-start.2
  1086.2 14.3 %all-gather.4 = bf16[8,2,8192]{2,1,0:T(2,128)(2,1)S(1)} all-gather(bf16[1,2,8192]{2,1,0:T(2,128)(2,1)S(1)} %bitcast.3423), channel_id=1, replica_groups=mesh['layer'=4,'row'=8] {'row'}, dimensions={0}, use_global_device_ids=true | all-gather | bytes 294912 | tf_op jit(solution)/shard_map/all_gather | solution.py:102
  1100.6 3.4 fusion.9
  1106.4 22.8 %fusion.7 = bf16[16,4096]{1,0:T(8,128)(2,1)S(1)} fusion(f32[16,4096]{1,0:T(8,128)S(1)} %fusion.316, bf16[16,8192]{1,0:T(8,128)(2,1)S(1)} %reshape.316, bf16[4096,8192]{0,1:T(8,128)(2,1)} %slice_dynamic-update-slice_fusion), kind=kOutput, calls=%fused_computation.29 | convolution fusion | flops 1073938432 | bytes 67764224 | tf_op jit(solution)/shard_map/dot_general | solution.py:70
  1130.0 3.4 all-to-all-start.3
  1134.7 4.1 copy.22
  (2073 shorter events, 654.4 us)
Async XLA Ops:
  7.2 113.0 %all-gather.7.cloned.1.call-start = ((), (), s32[]{:S(2)}) async-start(), calls=%async_computation.4 | async-start | bytes 4718592 | tf_op jit(solution)/shard_map/all_gather | solution.py:91
  15.0 79.7 %copy-start.472 = (bf16[2,8192]{1,0:T(2,128)(2,1)S(1)}, bf16[2,8192]{1,0:T(2,128)(2,1)}, u32[]{:S(2)}) copy-start(bf16[2,8192]{1,0:T(2,128)(2,1)} %param.4) | copy-start | bytes 98308
  127.3 106.5 %copy-start.486 = (f32[16]{0:T(128)}, f32[16]{0:T(128)S(1)}, u32[]{:S(2)}) copy-start(f32[16]{0:T(128)S(1)} %get-tuple-element.247) | copy-start | bytes 196
  127.3 106.6 %copy-start.505 = (f32[16]{0:T(128)}, f32[16]{0:T(128)S(1)}, u32[]{:S(2)}) copy-start(f32[16]{0:T(128)S(1)} %get-tuple-element.246) | copy-start | bytes 196
  127.3 106.6 %copy-start.527 = (f32[16]{0:T(128)}, f32[16]{0:T(128)S(1)}, u32[]{:S(2)}) copy-start(f32[16]{0:T(128)S(1)} %get-tuple-element.245) | copy-start | bytes 196
  127.3 106.6 %copy-start.545 = (f32[16]{0:T(128)}, f32[16]{0:T(128)S(1)}, u32[]{:S(2)}) copy-start(f32[16]{0:T(128)S(1)} %get-tuple-element.244) | copy-start | bytes 196
  127.4 106.6 %copy-start.563 = (f32[16]{0:T(128)}, f32[16]{0:T(128)S(1)}, u32[]{:S(2)}) copy-start(f32[16]{0:T(128)S(1)} %get-tuple-element.243) | copy-start | bytes 196
  127.4 106.6 %copy-start.580 = (f32[16]{0:T(128)}, f32[16]{0:T(128)S(1)}, u32[]{:S(2)}) copy-start(f32[16]{0:T(128)S(1)} %get-tuple-element.242) | copy-start | bytes 196
  127.4 106.6 %copy-start.597 = (f32[16]{0:T(128)}, f32[16]{0:T(128)S(1)}, u32[]{:S(2)}) copy-start(f32[16]{0:T(128)S(1)} %get-tuple-element.241) | copy-start | bytes 196
  127.4 106.6 %copy-start.614 = (f32[16]{0:T(128)}, f32[16]{0:T(128)S(1)}, u32[]{:S(2)}) copy-start(f32[16]{0:T(128)S(1)} %get-tuple-element.240) | copy-start | bytes 196
  127.4 106.6 %copy-start.631 = (f32[16]{0:T(128)}, f32[16]{0:T(128)S(1)}, u32[]{:S(2)}) copy-start(f32[16]{0:T(128)S(1)} %get-tuple-element.239) | copy-start | bytes 196
  127.4 106.6 %copy-start.648 = (f32[16]{0:T(128)}, f32[16]{0:T(128)S(1)}, u32[]{:S(2)}) copy-start(f32[16]{0:T(128)S(1)} %get-tuple-element.238) | copy-start | bytes 196
  127.4 106.6 %copy-start.664 = (f32[16]{0:T(128)}, f32[16]{0:T(128)S(1)}, u32[]{:S(2)}) copy-start(f32[16]{0:T(128)S(1)} %get-tuple-element.237) | copy-start | bytes 196
  170.3 293.7 %copy-start.39 = (f32[4096,1]{0,1:T(1,128)}, f32[4096,1]{0,1:T(1,128)S(1)}, u32[]{:S(2)}) copy-start(f32[4096,1]{0,1:T(1,128)S(1)} %fusion.282) | copy-start | bytes 49156
  172.9 291.0 %copy-start.75 = (f32[4096,1]{0,1:T(1,128)}, f32[4096,1]{0,1:T(1,128)S(1)}, u32[]{:S(2)}) copy-start(f32[4096,1]{0,1:T(1,128)S(1)} %fusion.281) | copy-start | bytes 49156
  210.6 253.4 %copy-start.41 = (f32[4096,1]{0,1:T(1,128)}, f32[4096,1]{0,1:T(1,128)S(1)}, u32[]{:S(2)}) copy-start(f32[4096,1]{0,1:T(1,128)S(1)} %fusion.266) | copy-start | bytes 49156
  212.3 251.7 %copy-start.77 = (f32[4096,1]{0,1:T(1,128)}, f32[4096,1]{0,1:T(1,128)S(1)}, u32[]{:S(2)}) copy-start(f32[4096,1]{0,1:T(1,128)S(1)} %fusion.265) | copy-start | bytes 49156
  243.2 220.8 %copy-start.17 = (f32[4096,1]{0,1:T(1,128)}, f32[4096,1]{0,1:T(1,128)S(1)}, u32[]{:S(2)}) copy-start(f32[4096,1]{0,1:T(1,128)S(1)} %fusion.251) | copy-start | bytes 49156
  245.5 218.5 %copy-start.43 = (f32[4096,1]{0,1:T(1,128)}, f32[4096,1]{0,1:T(1,128)S(1)}, u32[]{:S(2)}) copy-start(f32[4096,1]{0,1:T(1,128)S(1)} %fusion.250) | copy-start | bytes 49156
  283.4 180.6 %copy-start.19 = (f32[4096,1]{0,1:T(1,128)}, f32[4096,1]{0,1:T(1,128)S(1)}, u32[]{:S(2)}) copy-start(f32[4096,1]{0,1:T(1,128)S(1)} %fusion.235) | copy-start | bytes 49156
  285.1 178.9 %copy-start.45 = (f32[4096,1]{0,1:T(1,128)}, f32[4096,1]{0,1:T(1,128)S(1)}, u32[]{:S(2)}) copy-start(f32[4096,1]{0,1:T(1,128)S(1)} %fusion.234) | copy-start | bytes 49156
  286.7 177.3 %copy-start.84 = (f32[4096,1]{0,1:T(1,128)}, f32[4096,1]{0,1:T(1,128)S(1)}, u32[]{:S(2)}) copy-start(f32[4096,1]{0,1:T(1,128)S(1)} %fusion.233) | copy-start | bytes 49156
  288.5 175.6 %copy-start.125 = (f32[4096,1]{0,1:T(1,128)}, f32[4096,1]{0,1:T(1,128)S(1)}, u32[]{:S(2)}) copy-start(f32[4096,1]{0,1:T(1,128)S(1)} %fusion.232) | copy-start | bytes 49156
  290.1 173.9 %copy-start.162 = (f32[4096,1]{0,1:T(1,128)}, f32[4096,1]{0,1:T(1,128)S(1)}, u32[]{:S(2)}) copy-start(f32[4096,1]{0,1:T(1,128)S(1)} %fusion.231) | copy-start | bytes 49156
  291.9 172.1 %copy-start.194 = (f32[4096,1]{0,1:T(1,128)}, f32[4096,1]{0,1:T(1,128)S(1)}, u32[]{:S(2)}) copy-start(f32[4096,1]{0,1:T(1,128)S(1)} %fusion.230) | copy-start | bytes 49156
  313.9 150.1 %copy-start.21 = (f32[4096,1]{0,1:T(1,128)}, f32[4096,1]{0,1:T(1,128)S(1)}, u32[]{:S(2)}) copy-start(f32[4096,1]{0,1:T(1,128)S(1)} %fusion.219) | copy-start | bytes 49156
  315.6 148.5 %copy-start.48 = (f32[4096,1]{0,1:T(1,128)}, f32[4096,1]{0,1:T(1,128)S(1)}, u32[]{:S(2)}) copy-start(f32[4096,1]{0,1:T(1,128)S(1)} %fusion.218) | copy-start | bytes 49156
  317.2 146.8 %copy-start.87 = (f32[4096,1]{0,1:T(1,128)}, f32[4096,1]{0,1:T(1,128)S(1)}, u32[]{:S(2)}) copy-start(f32[4096,1]{0,1:T(1,128)S(1)} %fusion.217) | copy-start | bytes 49156
  319.0 145.1 %copy-start.128 = (f32[4096,1]{0,1:T(1,128)}, f32[4096,1]{0,1:T(1,128)S(1)}, u32[]{:S(2)}) copy-start(f32[4096,1]{0,1:T(1,128)S(1)} %fusion.216) | copy-start | bytes 49156
  320.7 143.4 %copy-start.164 = (f32[4096,1]{0,1:T(1,128)}, f32[4096,1]{0,1:T(1,128)S(1)}, u32[]{:S(2)}) copy-start(f32[4096,1]{0,1:T(1,128)S(1)} %fusion.215) | copy-start | bytes 49156
  322.4 141.7 %copy-start.196 = (f32[4096,1]{0,1:T(1,128)}, f32[4096,1]{0,1:T(1,128)S(1)}, u32[]{:S(2)}) copy-start(f32[4096,1]{0,1:T(1,128)S(1)} %fusion.214) | copy-start | bytes 49156
  344.3 119.8 %copy-start.23 = (f32[4096,1]{0,1:T(1,128)}, f32[4096,1]{0,1:T(1,128)S(1)}, u32[]{:S(2)}) copy-start(f32[4096,1]{0,1:T(1,128)S(1)} %fusion.203) | copy-start | bytes 49156
  346.1 118.0 %copy-start.51 = (f32[4096,1]{0,1:T(1,128)}, f32[4096,1]{0,1:T(1,128)S(1)}, u32[]{:S(2)}) copy-start(f32[4096,1]{0,1:T(1,128)S(1)} %fusion.202) | copy-start | bytes 49156
  347.8 116.3 %copy-start.90 = (f32[4096,1]{0,1:T(1,128)}, f32[4096,1]{0,1:T(1,128)S(1)}, u32[]{:S(2)}) copy-start(f32[4096,1]{0,1:T(1,128)S(1)} %fusion.201) | copy-start | bytes 49156
  349.5 114.6 %copy-start.131 = (f32[4096,1]{0,1:T(1,128)}, f32[4096,1]{0,1:T(1,128)S(1)}, u32[]{:S(2)}) copy-start(f32[4096,1]{0,1:T(1,128)S(1)} %fusion.200) | copy-start | bytes 49156
  351.2 112.9 %copy-start.166 = (f32[4096,1]{0,1:T(1,128)}, f32[4096,1]{0,1:T(1,128)S(1)}, u32[]{:S(2)}) copy-start(f32[4096,1]{0,1:T(1,128)S(1)} %fusion.199) | copy-start | bytes 49156
  353.0 111.2 %copy-start.198 = (f32[4096,1]{0,1:T(1,128)}, f32[4096,1]{0,1:T(1,128)S(1)}, u32[]{:S(2)}) copy-start(f32[4096,1]{0,1:T(1,128)S(1)} %fusion.198) | copy-start | bytes 49156
  354.8 109.3 %copy-start.232 = (f32[4096,1]{0,1:T(1,128)}, f32[4096,1]{0,1:T(1,128)S(1)}, u32[]{:S(2)}) copy-start(f32[4096,1]{0,1:T(1,128)S(1)} %fusion.197) | copy-start | bytes 49156
  385.2 79.0 %copy-start.25 = (f32[4096,1]{0,1:T(1,128)}, f32[4096,1]{0,1:T(1,128)S(1)}, u32[]{:S(2)}) copy-start(f32[4096,1]{0,1:T(1,128)S(1)} %fusion.187) | copy-start | bytes 49156
  386.9 77.3 %copy-start.54 = (f32[4096,1]{0,1:T(1,128)}, f32[4096,1]{0,1:T(1,128)S(1)}, u32[]{:S(2)}) copy-start(f32[4096,1]{0,1:T(1,128)S(1)} %fusion.186) | copy-start | bytes 49156
  388.7 75.5 %copy-start.93 = (f32[4096,1]{0,1:T(1,128)}, f32[4096,1]{0,1:T(1,128)S(1)}, u32[]{:S(2)}) copy-start(f32[4096,1]{0,1:T(1,128)S(1)} %fusion.185) | copy-start | bytes 49156
  928.2 11.1 all-to-all-start
  946.0 5.8 collective-permute-start
  1001.6 11.2 all-to-all-start.1
  1019.5 5.5 collective-permute-start.1
  1068.8 10.1 all-to-all-start.2
  1079.9 6.3 collective-permute-start.2
  1130.0 10.1 all-to-all-start.3
  (685 other events, 10740.4 us)
Sparse Core Ops, SparseCore 0:
  9.6 49.8 all-gather.6
where the time goes:
time: 1170 us; the launch traced here: 1150 us
  other arithmetic  600 us (51%)
  local copies, waits for them, and re-layouts  273 us (23%)
  matrix products  146 us (12%)
  blocking collectives  59.6 us (5%)
  between operations  27.4 us (2%)
  starting transfers between devices  26.9 us (2%)
  waiting for transfers between devices  15.4 us (1%)
    mul x256, other arithmetic, eliminate(): current[:, offset:offset + 1] * dropped[:, index_col:index_col + 1]  413 us
    unnamed x1457, local copies, waits for them, and re-layouts  101 us
    sub x240, other arithmetic, eliminate(): current - error * pivot_block[index_col:index_col + 1, start:finish]  99.2 us
    dot_general x4, matrix products, transposed_dot(): lax.dot_general(left, right, (((1,), (1,)), ((), ())), preferred_element_...  94.6 us
    unnamed x31, other arithmetic  62.7 us
    all_gather x4, blocking collectives, per_device(): portion = lax.all_gather(section_input, 'row', axis=0, tiled=True)  59.6 us
    concatenate x1, local copies, waits for them, and re-layouts, prune_layer(): return (pruned, jnp.concatenate([errors_first, errors_second], 1))  50.6 us
    concatenate x1, local copies, waits for them, and re-layouts, per_device(): mixed_weight = jnp.concatenate([pruned, weight[:, leading_count:]], 1)  43.2 us
  transfers between devices with their start and end apart: 8, of which 4 were waited for; matrix products, arithmetic and copies ran while one was open for 10% of the time, Pallas kernels for 0%

commit v1 on v0

v1 whole, which is shorter than its diff:
```python
import functools

import jax
import jax.numpy as jnp
from jax import lax
from jax.experimental import pallas as pl
from jax.experimental.pallas import tpu as pltpu
from jax.sharding import PartitionSpec as P

BLOCK = 128
SUB = 16

epsilon = 1e-05


def passed_along(array, axis, by):
    size = lax.axis_size(axis)
    pairs = [(i, i + by) for i in range(size) if 0 <= i + by < size]
    return lax.ppermute(array, axis, pairs)


def gathered(array, axis):
    size = lax.axis_size(axis)
    copies = jnp.broadcast_to(array[None], (size,) + array.shape)
    return lax.all_to_all(copies, axis, split_axis=0, concat_axis=0)


def nt_dot(left, right):
    return lax.dot_general(
        left, right, (((1,), (1,)), ((), ())), preferred_element_type=jnp.float32
    )


def nn_dot(left, right):
    return jnp.dot(left, right, preferred_element_type=jnp.float32)


def split_halves(value):
    high = value.astype(jnp.bfloat16)
    low = (value - high.astype(jnp.float32)).astype(jnp.bfloat16)
    return high, low


def identity(count):
    row = lax.broadcasted_iota(jnp.int32, (count, count), 0)
    column = lax.broadcasted_iota(jnp.int32, (count, count), 1)
    return jnp.where(row == column, 1.0, 0.0).astype(jnp.bfloat16)


def eliminate_kernel(scalar_ref, inverse_ref, inner_ref, cross_ref, weight_ref, mask_ref,
                     pruned_ref, aux_ref, state, dropped, errors):
    count = 2 * BLOCK
    depth = count * 8
    sheets = state.shape[0] // depth
    lanes = sheets * 128
    spots = [(g, q, slice((g * sheets + q) * 128, (g * sheets + q + 1) * 128))
             for g in range(8) for q in range(sheets)]

    def place(g, q, first, size):
        return pl.ds(q * depth + first * 8 + g, size, stride=8)

    def plane(q, j):
        return slice(q * depth + j * 8, q * depth + (j + 1) * 8)

    eye = identity(count)
    columns = nt_dot(eye, weight_ref[...])
    drops = nt_dot(eye, (1 - mask_ref[...]).astype(jnp.float32).astype(jnp.bfloat16))
    for g, q, where in spots:
        state[place(g, q, 0, count), :] = columns[:, where]
        dropped[place(g, q, 0, count), :] = drops[:, where]

    def stacked(first, size):
        wide = jnp.concatenate([errors[place(g, q, first, size), :] for g, q, _ in spots], 1)
        return jnp.concatenate(split_halves(wide), 0)

    def subtract(product, first, size):
        for g, q, where in spots:
            at = place(g, q, first, size)
            state[at, :] = state[at, :] - product[:, where]

    for block in range(2):
        for part in range(BLOCK // SUB):
            first = block * BLOCK + part * SUB
            planes = [[state[plane(q, first + i), :] for q in range(sheets)] for i in range(SUB)]
            for i in range(SUB):
                j = first + i
                inverse = inverse_ref[j]
                error = []
                for q in range(sheets):
                    lost = planes[i][q] * dropped[plane(q, j), :]
                    error.append(lost * inverse)
                    state[plane(q, j), :] = planes[i][q] - lost
                    errors[plane(q, j), :] = error[q]
                for k in range(i + 1, SUB):
                    scalar = scalar_ref[j * SUB + k]
                    for q in range(sheets):
                        planes[k][q] = planes[k][q] - error[q] * scalar
            after = first + SUB
            left = (block + 1) * BLOCK - after
            if left:
                factor = inner_ref[block * (BLOCK // SUB) + part, after : after + left, :]
                subtract(nn_dot(factor, stacked(first, SUB)), after, left)
        if block == 0:
            subtract(nn_dot(cross_ref[...], stacked(0, BLOCK)), BLOCK, BLOCK)

    small = identity(128)
    for g, q, where in spots:
        kept = state[place(g, q, 0, count), :].astype(jnp.bfloat16)
        high, low = split_halves(errors[place(g, q, 0, count), :])
        aux_ref[0:count, where] = kept
        aux_ref[count : 2 * count, where] = high
        aux_ref[2 * count : 3 * count, where] = low
        pruned_ref[where, :] = nt_dot(small, kept).astype(jnp.bfloat16)


def eliminate(weight, factor, mask):
    count = 2 * BLOCK
    given = weight.shape[0]
    rows = pl.cdiv(given, 1024) * 1024
    if rows != given:
        more = ((0, rows - given), (0, 0))
        weight, mask = jnp.pad(weight[:, :count], more), jnp.pad(mask, more)
    tile = 1024 if rows % 2048 else 2048
    subs = count // SUB
    wide = factor.astype(jnp.float32)
    row = lax.broadcasted_iota(jnp.int32, wide.shape, 0)
    column = lax.broadcasted_iota(jnp.int32, wide.shape, 1)
    inverse = 1.0 / jnp.sum(jnp.where(row == column, wide, 0.0), axis=1)
    near = jnp.where(row // SUB == column // SUB, wide, 0.0)
    scalars = near.reshape(count, subs, SUB).sum(axis=1).reshape(-1)
    columns = factor.T.reshape(count, subs, SUB).transpose(1, 0, 2)
    inner = jnp.concatenate([columns, columns], 2)
    cross = factor[:BLOCK, BLOCK:].T
    cross = jnp.concatenate([cross, cross], 1)
    smem = pl.BlockSpec(memory_space=pltpu.SMEM)
    pruned, aux = pl.pallas_call(
        eliminate_kernel,
        grid=(rows // tile,),
        in_specs=[
            smem,
            smem,
            pl.BlockSpec((subs, count, 2 * SUB), lambda i: (0, 0, 0)),
            pl.BlockSpec((BLOCK, count), lambda i: (0, 0)),
            pl.BlockSpec((tile, count), lambda i: (i, 0)),
            pl.BlockSpec((tile, count), lambda i: (i, 0)),
        ],
        out_specs=[
            pl.BlockSpec((tile, count), lambda i: (i, 0)),
            pl.BlockSpec((3 * count, tile), lambda i: (0, i)),
        ],
        out_shape=[
            jax.ShapeDtypeStruct((rows, count), jnp.bfloat16),
            jax.ShapeDtypeStruct((3 * count, rows), jnp.bfloat16),
        ],
        scratch_shapes=[pltpu.VMEM((tile * count // 128, 128), jnp.float32)] * 3,
        compiler_params=pltpu.CompilerParams(vmem_limit_bytes=52 * 1024 * 1024),
        cost_estimate=pl.CostEstimate(
            flops=2 * rows * count * count, bytes_accessed=rows * count * 14, transcendentals=0
        ),
        name="eliminate",
    )(scalars, inverse, inner, cross, weight, mask)
    return pruned[:given], aux[:, :given]


def combine_kernel(scale, product_ref, lead_ref, panel_ref, aux_ref, out_ref):
    count = 2 * BLOCK
    tokens = product_ref.shape[0]
    high, low = split_halves(panel_ref[...])
    both = nn_dot(jnp.concatenate([high, low], 0), aux_ref[count : 2 * count, :])
    correction = both[:tokens] + both[tokens:] + nn_dot(high, aux_ref[2 * count :, :])
    pruned = nn_dot(lead_ref[...], aux_ref[0:count, :])
    out_ref[...] = ((product_ref[...] + pruned - correction) * scale).astype(jnp.bfloat16)


def combine(product, lead, panel_inputs, aux, scale):
    tokens, rows = product.shape
    count = 2 * BLOCK
    tile = min(1024, rows)
    return pl.pallas_call(
        functools.partial(combine_kernel, scale),
        grid=(rows // tile,),
        in_specs=[
            pl.BlockSpec((tokens, tile), lambda i: (0, i)),
            pl.BlockSpec((tokens, count), lambda i: (0, 0)),
            pl.BlockSpec((tokens, count), lambda i: (0, 0)),
            pl.BlockSpec((3 * count, tile), lambda i: (0, i)),
        ],
        out_specs=pl.BlockSpec((tokens, tile), lambda i: (0, i)),
        out_shape=jax.ShapeDtypeStruct((tokens, rows), jnp.bfloat16),
        compiler_params=pltpu.CompilerParams(vmem_limit_bytes=24 * 1024 * 1024),
        cost_estimate=pl.CostEstimate(
            flops=8 * tokens * rows * count, bytes_accessed=rows * count * 6, transcendentals=0
        ),
        name="combine",
    )(product, lead, panel_inputs, aux)


def per_device(tokens, up_weight, hess_panel, keep_mask):
    weight = up_weight[0]
    local_panel = hess_panel[0].astype(jnp.bfloat16)
    count = 2 * BLOCK
    features = weight.shape[1]
    row_size = lax.axis_size("row")
    own = tokens.shape[0]
    position = lax.axis_index("layer")
    depth = lax.axis_size("layer")

    width = min(count, local_panel.shape[1])
    share = count // row_size
    factor_share = local_panel[:, :width].reshape(row_size, share * width // count, count)
    token_share = jnp.broadcast_to(
        tokens.reshape(1, own * features // count, count), (row_size, own * features // count, count)
    )
    first = lax.all_to_all(
        jnp.concatenate([token_share, factor_share], 1), "row", split_axis=0, concat_axis=0
    )
    cut = own * features // count
    portion = first[:, :cut].reshape(row_size * own, features)
    owned = [first[o, cut:].reshape(share, width) for o in range(count // width)]
    factor = gathered(jnp.concatenate(owned, 1), "row").reshape(count, count)
    full_panel = lax.all_gather(local_panel, "row", axis=1, tiled=True)

    pruned, aux = eliminate(weight, factor, keep_mask[0])

    section_input = tokens
    results = jnp.zeros_like(tokens)
    for turn in range(depth):
        if turn:
            portion = gathered(section_input, "row").reshape(row_size * own, features)
        lead = portion[:, :count]
        column = lax.broadcasted_iota(jnp.int32, portion.shape, 1)
        rest = jnp.where(column < count, jnp.zeros_like(portion), portion)
        product = nt_dot(rest, weight)
        panel_inputs = nt_dot(rest, full_panel)
        layer_output = combine(product, lead, panel_inputs, aux, features ** (-0.5))
        spread = lax.all_to_all(layer_output, "row", split_axis=0, concat_axis=1, tiled=True)
        hidden = jax.nn.silu(spread.astype(jnp.float32))
        folded = hidden.reshape(own, -1, features).sum(axis=1)
        combined = section_input.astype(jnp.float32) + folded
        moment = jnp.mean(combined * combined, axis=-1, keepdims=True)
        produced = (combined * lax.rsqrt(moment + epsilon)).astype(jnp.bfloat16)
        results = jnp.where(position == turn, produced, results)
        if turn + 1 < depth:
            section_input = passed_along(produced, "layer", 1)
    return (results[None], pruned[None])


def solution(mesh):
    in_specs = (
        P("row", None),
        P("layer", "row", None),
        P("layer", None, "row"),
        P("layer", "row", None),
    )
    out_specs = (P("layer", "row", None), P("layer", "row", None))
    return jax.shard_map(
        per_device, mesh=mesh, in_specs=in_specs, out_specs=out_specs, check_vma=False
    )
```

time: 1170 us -> 313 us (0.27); the launches traced: 1150 us -> 310 us
  other arithmetic: 600 us -> 8.76 us
  local copies, waits for them, and re-layouts: 273 us -> 17.7 us
  matrix products: 146 us -> 115 us
  Pallas kernels: 0 us -> 27.6 us
  waiting for transfers between devices: 15.4 us -> 33.4 us
  between operations: 27.4 us -> 14.5 us
    mul x256 -> x0, other arithmetic: 413 us -> none  [eliminate(): current[:, offset:offset + 1] * dropped[:, index_col:index_col + 1]]
    concatenate x17 -> x1, local copies, waits for them, and re-layouts: 125 us -> 0.48 us  [eliminate(): inner = jnp.concatenate([columns, columns], 2)]
    sub x241 -> x0, other arithmetic: 104 us -> none  [the longest x240 99.2 us: eliminate(): current - error * pivot_block[index_col:index_col + 1, start:finish]]
    unnamed x1457 -> x11, local copies, waits for them, and re-layouts: 101 us -> 11.3 us
    all_to_all x0 -> x6, blocking collectives: none -> 66.8 us  [the longest x3 36.7 us: gathered(): return lax.all_to_all(copies, axis, split_axis=0, concat_axis=0)]
    unnamed x31 -> x0, other arithmetic: 62.7 us -> none
    all_gather x4 -> x0, blocking collectives: 59.6 us -> none  [per_device(): portion = lax.all_gather(section_input, 'row', axis=0, tiled=True)]
    dot_general x27 -> x8, matrix products: 146 us -> 115 us  [nt_dot(): lax.dot_general(left, right, (((1,), (1,)), ((), ())), preferred_element_...]
  transfers between devices with their start and end apart: 8 -> 7, of which waited for: 4 -> 5; matrix products, arithmetic and copies ran while one was open for 10% -> 10% of each run, Pallas kernels for 0% -> 7%
where the time goes in v1:
time: 313 us; the launch traced here: 310 us
  matrix products  115 us (37%)
  blocking collectives  66.8 us (21%)
  waiting for transfers between devices  33.4 us (11%)
  Pallas kernels  27.6 us (9%)
  starting transfers between devices  26.1 us (8%)
  local copies, waits for them, and re-layouts  17.7 us (6%)
  between operations  14.5 us (5%)
  other arithmetic  8.76 us (3%)
    dot_general x8, matrix products, nt_dot(): lax.dot_general(left, right, (((1,), (1,)), ((), ())), preferred_element_...  115 us
    all_to_all x3, blocking collectives, gathered(): return lax.all_to_all(copies, axis, split_axis=0, concat_axis=0)  36.7 us
    all_to_all x3, blocking collectives, per_device(): lax.all_to_all(layer_output, 'row', split_axis=0, concat_axis=1, tiled=True)  30.1 us
    all_to_all x1, waiting for transfers between devices, per_device(): lax.all_to_all(jnp.concatenate([token_share, factor_share], 1), 'row', sp...  21.9 us
    pallas_call x1, Pallas kernels, eliminate(): pl.pallas_call(eliminate_kernel, grid=(rows // tile,), in_specs=[smem, sm...  20.3 us
    ppermute x3, starting transfers between devices, passed_along(): return lax.ppermute(array, axis, pairs)  11.9 us
    unnamed x11, local copies, waits for them, and re-layouts  11.3 us
    pallas_call x4, Pallas kernels, combine(): pl.pallas_call(functools.partial(combine_kernel, scale), grid=(rows // ti...  7.31 us
  transfers between devices with their start and end apart: 7, of which 5 were waited for; matrix products, arithmetic and copies ran while one was open for 10% of the time, Pallas kernels for 7%

profile of v1, /device:TPU:0, one launch (start us, length us, event | category | flops | bytes accessed | tf_op | source)
XLA Modules:
  0.0 310.0 jit_solution(5916493863408440322)
XLA Ops:
  7.2 2.1 convert_element_type.81
  9.4 1.3 convert_bitcast_fusion.4
  10.7 0.8 broadcast_in_dim.52
  11.5 0.8 pad_maximum_fusion
  12.3 6.3 %all-to-all-start = ((bf16[8,96,256]{2,1,0:T(8,128)(2,1)}), bf16[8,96,256]{2,1,0:T(8,128)(2,1)S(1)}, u32[]{:S(2)}, u32[]{:S(2)}) async-start(bf16[8,96,256]{2,1,0:T(8,128)(2,1)} %pad_maximum_fusion), calls=%async_computation | async-start | bytes 786432 | tf_op jit(solution)/shard_map/all_to_all | solution.py:214
  18.7 21.9 %all-to-all-done = bf16[8,96,256]{2,1,0:T(8,128)(2,1)S(1)} async-done(((bf16[8,96,256]{2,1,0:T(8,128)(2,1)}), bf16[8,96,256]{2,1,0:T(8,128)(2,1)S(1)}, u32[]{:S(2)}, u32[]{:S(2)}) %all-to-all-start) | async-done | bytes 393248 | tf_op jit(solution)/shard_map/all_to_all | solution.py:214
  40.6 0.7 broadcast_in_dim.55
  41.3 4.4 %all-to-all-start.1 = ((bf16[8,32,256]{2,1,0:T(8,128)(2,1)}), bf16[8,32,256]{2,1,0:T(8,128)(2,1)S(1)}, u32[]{:S(2)}, u32[]{:S(2)}) async-start(bf16[8,32,256]{2,1,0:T(8,128)(2,1)} %broadcast_in_dim.55), calls=%async_computation.1 | async-start | bytes 262144 | tf_op jit(solution)/shard_map/all_to_all | solution.py:25
  45.9 25.6 %fusion.33.product_ref = f32[16,4096]{1,0:T(8,128)S(1)} fusion(bf16[16,8192]{1,0:T(8,128)(2,1)S(1)} %select_n.80, bf16[1,4096,8192]{2,1,0:T(8,128)(2,1)} %param.5), kind=kOutput, calls=%fused_computation.86 | convolution fusion | flops 1073741824 | bytes 67633152 | tf_op jit(solution)/shard_map/dot_general | solution.py:29
  71.7 0.3 copy.15
  72.0 0.3 reshape.176
  72.7 0.5 copy.18.inner_ref
  73.6 20.3 %eliminate.1 = (bf16[4096,256]{1,0:T(8,128)(2,1)}, bf16[768,4096]{1,0:T(8,128)(2,1)}) custom-call(f32[4096]{0:T(1024)S(1)} %reshape.170.scalar_ref, f32[256]{0:T(256)S(1)} %div.59.inverse_ref, bf16[16,256,32]{2,1,0:T(8,128)(2,1)S(1)} %copy.18.inner_ref, bf16[128,256]{1,0:T(8,128)(2,1)S(1)} %pad_maximum_fusion.2.cross_ref, ...), custom_call_target="tpu_custom_call" | custom-call | flops 536870912 | bytes 14680064 | tf_op jit(solution)/shard_map/eliminate/pallas_call | solution.py:136
  93.9 3.4 %fusion.6.panel_ref = f32[16,256]{1,0:T(8,128)S(1)} fusion(bf16[1,256,8192]{2,1,0:T(8,128)(2,1)} %all-gather.3.cloned.1.call-done, bf16[16,8192]{1,0:T(8,128)(2,1)S(1)} %reshape.169, pred[8192]{0:T(1024)(128)(4,1)S(1)} %iota_compare_fusion.1), kind=kOutput, calls=%fused_computation.6 | convolution fusion | flops 67239936 | bytes 4481024 | tf_op jit(solution)/shard_map/dot_general | solution.py:29
  97.3 2.8 copy-done
  100.1 1.8 combine.4
  102.0 11.8 %all_to_all.77 = bf16[8,2,4096]{2,1,0:T(2,128)(2,1)S(1)} all-to-all(bf16[8,2,4096]{2,1,0:T(2,128)(2,1)S(1)} %all_to_all.57), channel_id=1, replica_groups=mesh['layer'=4,'row'=8] {'row'}, dimensions={0} | all-to-all | bytes 262144 | tf_op jit(solution)/shard_map/all_to_all | solution.py:236
  114.2 0.3 fusion.12
  114.8 3.4 %collective-permute-start = (bf16[2,8192]{1,0:T(2,128)(2,1)S(1)}, bf16[2,8192]{1,0:T(2,128)(2,1)S(1)}, u32[]{:S(2)}, u32[]{:S(2)}) collective-permute-start(bf16[2,8192]{1,0:T(2,128)(2,1)S(1)} %multiply_convert_fusion.3), channel_id=1, source_target_pairs={{0,8},{8,16},{16,24},{1,9},{9,17},{17,25},{2,10},{10,18},{18,26},{... | collective-permute-start | bytes 98312 | tf_op jit(solution)/shard_map/ppermute | solution.py:19
  118.2 1.6 collective-permute-done
  119.9 12.2 %all_to_all.78 = bf16[8,2,8192]{2,1,0:T(2,128)(2,1)S(1)} all-to-all(bf16[8,2,8192]{2,1,0:T(2,128)(2,1)S(1)} %broadcast_in_dim.58), channel_id=1, replica_groups=mesh['layer'=4,'row'=8] {'row'}, dimensions={0} | all-to-all | bytes 524288 | tf_op jit(solution)/shard_map/all_to_all | solution.py:25
  132.5 25.4 %fusion.31.product_ref = f32[16,4096]{1,0:T(8,128)S(1)} fusion(bf16[16,8192]{1,0:T(8,128)(2,1)S(1)} %select_n.87, bf16[1,4096,8192]{2,1,0:T(8,128)(2,1)} %param.5), kind=kOutput, calls=%fused_computation.84 | convolution fusion | flops 1073741824 | bytes 67633152 | tf_op jit(solution)/shard_map/dot_general | solution.py:29
  158.0 3.4 %fusion.4.panel_ref = f32[16,256]{1,0:T(8,128)S(1)} fusion(bf16[1,256,8192]{2,1,0:T(8,128)(2,1)} %all-gather.3.cloned.1.call-done, bf16[16,8192]{1,0:T(8,128)(2,1)S(1)} %reshape.173, pred[8192]{0:T(1024)(128)(4,1)S(1)} %iota_compare_fusion.1), kind=kOutput, calls=%fused_computation.4 | convolution fusion | flops 67239936 | bytes 4481024 | tf_op jit(solution)/shard_map/dot_general | solution.py:29
  161.4 2.8 copy-done.1
  164.2 1.8 combine.5
  166.1 9.2 %all_to_all.79 = bf16[8,2,4096]{2,1,0:T(2,128)(2,1)S(1)} all-to-all(bf16[8,2,4096]{2,1,0:T(2,128)(2,1)S(1)} %all_to_all.60), channel_id=1, replica_groups=mesh['layer'=4,'row'=8] {'row'}, dimensions={0} | all-to-all | bytes 262144 | tf_op jit(solution)/shard_map/all_to_all | solution.py:236
  175.7 0.3 fusion.13
  176.3 4.2 %collective-permute-start.1 = (bf16[2,8192]{1,0:T(2,128)(2,1)S(1)}, bf16[2,8192]{1,0:T(2,128)(2,1)S(1)}, u32[]{:S(2)}, u32[]{:S(2)}) collective-permute-start(bf16[2,8192]{1,0:T(2,128)(2,1)S(1)} %multiply_convert_fusion.2), channel_id=1, source_target_pairs={{0,8},{8,16},{16,24},{1,9},{9,17},{17,25},{2,10},{10,18},{18,26},{... | collective-permute-start | bytes 98312 | tf_op jit(solution)/shard_map/ppermute | solution.py:19
  180.5 1.6 collective-permute-done.1
  182.2 12.2 %all_to_all.80 = bf16[8,2,8192]{2,1,0:T(2,128)(2,1)S(1)} all-to-all(bf16[8,2,8192]{2,1,0:T(2,128)(2,1)S(1)} %broadcast_in_dim.59), channel_id=1, replica_groups=mesh['layer'=4,'row'=8] {'row'}, dimensions={0} | all-to-all | bytes 524288 | tf_op jit(solution)/shard_map/all_to_all | solution.py:25
  194.8 25.4 %fusion.29.product_ref = f32[16,4096]{1,0:T(8,128)S(1)} fusion(bf16[16,8192]{1,0:T(8,128)(2,1)S(1)} %select_n.90, bf16[1,4096,8192]{2,1,0:T(8,128)(2,1)} %param.5), kind=kOutput, calls=%fused_computation.82 | convolution fusion | flops 1073741824 | bytes 67633152 | tf_op jit(solution)/shard_map/dot_general | solution.py:29
  220.3 3.4 %fusion.2.panel_ref = f32[16,256]{1,0:T(8,128)S(1)} fusion(bf16[1,256,8192]{2,1,0:T(8,128)(2,1)} %all-gather.3.cloned.1.call-done, bf16[16,8192]{1,0:T(8,128)(2,1)S(1)} %reshape.174, pred[8192]{0:T(1024)(128)(4,1)S(1)} %iota_compare_fusion.1), kind=kOutput, calls=%fused_computation.2 | convolution fusion | flops 67239936 | bytes 4481024 | tf_op jit(solution)/shard_map/dot_general | solution.py:29
  223.7 2.8 copy-done.2
  226.5 1.8 combine.6
  228.5 9.2 %all_to_all.81 = bf16[8,2,4096]{2,1,0:T(2,128)(2,1)S(1)} all-to-all(bf16[8,2,4096]{2,1,0:T(2,128)(2,1)S(1)} %all_to_all.63), channel_id=1, replica_groups=mesh['layer'=4,'row'=8] {'row'}, dimensions={0} | all-to-all | bytes 262144 | tf_op jit(solution)/shard_map/all_to_all | solution.py:236
  238.0 0.3 fusion.14
  238.6 4.3 %collective-permute-start.2 = (bf16[2,8192]{1,0:T(2,128)(2,1)S(1)}, bf16[2,8192]{1,0:T(2,128)(2,1)S(1)}, u32[]{:S(2)}, u32[]{:S(2)}) collective-permute-start(bf16[2,8192]{1,0:T(2,128)(2,1)S(1)} %multiply_convert_fusion.1), channel_id=1, source_target_pairs={{0,8},{8,16},{16,24},{1,9},{9,17},{17,25},{2,10},{10,18},{18,26},{... | collective-permute-start | bytes 98312 | tf_op jit(solution)/shard_map/ppermute | solution.py:19
  242.9 1.6 collective-permute-done.2
  244.6 12.2 %all_to_all.82 = bf16[8,2,8192]{2,1,0:T(2,128)(2,1)S(1)} all-to-all(bf16[8,2,8192]{2,1,0:T(2,128)(2,1)S(1)} %broadcast_in_dim.60), channel_id=1, replica_groups=mesh['layer'=4,'row'=8] {'row'}, dimensions={0} | all-to-all | bytes 524288 | tf_op jit(solution)/shard_map/all_to_all | solution.py:25
  257.2 25.4 %fusion.27.product_ref = f32[16,4096]{1,0:T(8,128)S(1)} fusion(bf16[16,8192]{1,0:T(8,128)(2,1)S(1)} %select_n.93, bf16[1,4096,8192]{2,1,0:T(8,128)(2,1)} %param.5), kind=kOutput, calls=%fused_computation.80 | convolution fusion | flops 1073741824 | bytes 67633152 | tf_op jit(solution)/shard_map/dot_general | solution.py:29
  282.8 3.4 %fusion.panel_ref = f32[16,256]{1,0:T(8,128)S(1)} fusion(bf16[1,256,8192]{2,1,0:T(8,128)(2,1)} %all-gather.3.cloned.1.call-done, bf16[16,8192]{1,0:T(8,128)(2,1)S(1)} %reshape.175, pred[8192]{0:T(1024)(128)(4,1)S(1)} %iota_compare_fusion.1), kind=kOutput, calls=%fused_computation | convolution fusion | flops 67239936 | bytes 4481024 | tf_op jit(solution)/shard_map/dot_general | solution.py:29
  286.1 2.8 copy-done.3
  288.9 1.8 combine.7
  290.8 0.7 all_to_all.66
  291.5 3.4 %all-to-all-start.8 = ((bf16[8,2,4096]{2,1,0:T(2,128)(2,1)}), bf16[8,2,4096]{2,1,0:T(2,128)(2,1)S(1)}, u32[]{:S(2)}, u32[]{:S(2)}) async-start(bf16[8,2,4096]{2,1,0:T(2,128)(2,1)} %all_to_all.66), calls=%async_computation.8 | async-start | bytes 262144 | tf_op jit(solution)/shard_map/all_to_all | solution.py:236
  294.9 6.7 %all-to-all-done.8 = bf16[8,2,4096]{2,1,0:T(2,128)(2,1)S(1)} async-done(((bf16[8,2,4096]{2,1,0:T(2,128)(2,1)}), bf16[8,2,4096]{2,1,0:T(2,128)(2,1)S(1)}, u32[]{:S(2)}, u32[]{:S(2)}) %all-to-all-start.8) | async-done | bytes 131104 | tf_op jit(solution)/shard_map/all_to_all | solution.py:236
  302.0 0.3 fusion.15
  302.5 0.7 fusion.24
  (76 shorter events, 6.0 us)
Async XLA Ops:
  7.2 86.7 %all-gather.3.cloned.1.call-start = ((), (), s32[]{:S(2)}) async-start(), calls=%async_computation.9 | async-start | bytes 4718592 | tf_op jit(solution)/shard_map/all_gather | solution.py:221
  12.3 28.3 %all-to-all-start = ((bf16[8,96,256]{2,1,0:T(8,128)(2,1)}), bf16[8,96,256]{2,1,0:T(8,128)(2,1)S(1)}, u32[]{:S(2)}, u32[]{:S(2)}) async-start(bf16[8,96,256]{2,1,0:T(8,128)(2,1)} %pad_maximum_fusion), calls=%async_computation | async-start | bytes 786432 | tf_op jit(solution)/shard_map/all_to_all | solution.py:214
  41.3 30.4 %all-to-all-start.1 = ((bf16[8,32,256]{2,1,0:T(8,128)(2,1)}), bf16[8,32,256]{2,1,0:T(8,128)(2,1)S(1)}, u32[]{:S(2)}, u32[]{:S(2)}) async-start(bf16[8,32,256]{2,1,0:T(8,128)(2,1)} %broadcast_in_dim.55), calls=%async_computation.1 | async-start | bytes 262144 | tf_op jit(solution)/shard_map/all_to_all | solution.py:25
  97.3 2.8 copy-start
  100.1 14.4 %copy-start.4 = (bf16[2,8192]{1,0:T(2,128)(2,1)S(1)}, bf16[2,8192]{1,0:T(2,128)(2,1)}, u32[]{:S(2)}) copy-start(bf16[2,8192]{1,0:T(2,128)(2,1)} %param.4) | copy-start | bytes 98308
  114.8 5.0 %collective-permute-start = (bf16[2,8192]{1,0:T(2,128)(2,1)S(1)}, bf16[2,8192]{1,0:T(2,128)(2,1)S(1)}, u32[]{:S(2)}, u32[]{:S(2)}) collective-permute-start(bf16[2,8192]{1,0:T(2,128)(2,1)S(1)} %multiply_convert_fusion.3), channel_id=1, source_target_pairs={{0,8},{8,16},{16,24},{1,9},{9,17},{17,25},{2,10},{10,18},{18,26},{... | collective-permute-start | bytes 98312 | tf_op jit(solution)/shard_map/ppermute | solution.py:19
  161.4 2.8 copy-start.1
  176.3 5.8 %collective-permute-start.1 = (bf16[2,8192]{1,0:T(2,128)(2,1)S(1)}, bf16[2,8192]{1,0:T(2,128)(2,1)S(1)}, u32[]{:S(2)}, u32[]{:S(2)}) collective-permute-start(bf16[2,8192]{1,0:T(2,128)(2,1)S(1)} %multiply_convert_fusion.2), channel_id=1, source_target_pairs={{0,8},{8,16},{16,24},{1,9},{9,17},{17,25},{2,10},{10,18},{18,26},{... | collective-permute-start | bytes 98312 | tf_op jit(solution)/shard_map/ppermute | solution.py:19
  223.7 2.8 copy-start.2
  238.6 5.9 %collective-permute-start.2 = (bf16[2,8192]{1,0:T(2,128)(2,1)S(1)}, bf16[2,8192]{1,0:T(2,128)(2,1)S(1)}, u32[]{:S(2)}, u32[]{:S(2)}) collective-permute-start(bf16[2,8192]{1,0:T(2,128)(2,1)S(1)} %multiply_convert_fusion.1), channel_id=1, source_target_pairs={{0,8},{8,16},{16,24},{1,9},{9,17},{17,25},{2,10},{10,18},{18,26},{... | collective-permute-start | bytes 98312 | tf_op jit(solution)/shard_map/ppermute | solution.py:19
  286.1 2.8 copy-start.3
  291.5 10.1 %all-to-all-start.8 = ((bf16[8,2,4096]{2,1,0:T(2,128)(2,1)}), bf16[8,2,4096]{2,1,0:T(2,128)(2,1)S(1)}, u32[]{:S(2)}, u32[]{:S(2)}) async-start(bf16[8,2,4096]{2,1,0:T(2,128)(2,1)} %all_to_all.66), calls=%async_computation.8 | async-start | bytes 262144 | tf_op jit(solution)/shard_map/all_to_all | solution.py:236
Sparse Core Ops, SparseCore 0:
  9.6 59.8 all-gather.2

commit v2 on v1

--- a/solution.py
+++ b/solution.py
@@ -106,10 +106,8 @@
     small = identity(128)
     for g, q, where in spots:
         kept = state[place(g, q, 0, count), :].astype(jnp.bfloat16)
-        high, low = split_halves(errors[place(g, q, 0, count), :])
         aux_ref[0:count, where] = kept
-        aux_ref[count : 2 * count, where] = high
-        aux_ref[2 * count : 3 * count, where] = low
+        aux_ref[count:, where] = errors[place(g, q, 0, count), :].astype(jnp.bfloat16)
         pruned_ref[where, :] = nt_dot(small, kept).astype(jnp.bfloat16)
 
 
@@ -146,30 +144,32 @@
         ],
         out_specs=[
             pl.BlockSpec((tile, count), lambda i: (i, 0)),
-            pl.BlockSpec((3 * count, tile), lambda i: (0, i)),
+            pl.BlockSpec((2 * count, tile), lambda i: (0, i)),
         ],
         out_shape=[
             jax.ShapeDtypeStruct((rows, count), jnp.bfloat16),
-            jax.ShapeDtypeStruct((3 * count, rows), jnp.bfloat16),
+            jax.ShapeDtypeStruct((2 * count, rows), jnp.bfloat16),
         ],
         scratch_shapes=[pltpu.VMEM((tile * count // 128, 128), jnp.float32)] * 3,
-        compiler_params=pltpu.CompilerParams(vmem_limit_bytes=52 * 1024 * 1024),
+        compiler_params=pltpu.CompilerParams(vmem_limit_bytes=26 * 1024 * 1024),
         cost_estimate=pl.CostEstimate(
-            flops=2 * rows * count * count, bytes_accessed=rows * count * 14, transcendentals=0
+            flops=2 * rows * count * count, bytes_accessed=rows * count * 12, transcendentals=0
         ),
         name="eliminate",
     )(scalars, inverse, inner, cross, weight, mask)
     return pruned[:given], aux[:, :given]
 
 
+def corrected(lead, panel_inputs, aux_ref, place):
+    count = 2 * BLOCK
+    tokens = lead.shape[0]
+    both = nn_dot(jnp.concatenate(split_halves(panel_inputs), 0), aux_ref[count:, place])
+    return nn_dot(lead, aux_ref[0:count, place]) - both[:tokens] - both[tokens:]
+
+
 def combine_kernel(scale, product_ref, lead_ref, panel_ref, aux_ref, out_ref):
-    count = 2 * BLOCK
-    tokens = product_ref.shape[0]
-    high, low = split_halves(panel_ref[...])
-    both = nn_dot(jnp.concatenate([high, low], 0), aux_ref[count : 2 * count, :])
-    correction = both[:tokens] + both[tokens:] + nn_dot(high, aux_ref[2 * count :, :])
-    pruned = nn_dot(lead_ref[...], aux_ref[0:count, :])
-    out_ref[...] = ((product_ref[...] + pruned - correction) * scale).astype(jnp.bfloat16)
+    change = corrected(lead_ref[...], panel_ref[...], aux_ref, slice(None))
+    out_ref[...] = ((product_ref[...] + change) * scale).astype(jnp.bfloat16)
 
 
 def combine(product, lead, panel_inputs, aux, scale):
@@ -183,43 +183,178 @@
             pl.BlockSpec((tokens, tile), lambda i: (0, i)),
             pl.BlockSpec((tokens, count), lambda i: (0, 0)),
             pl.BlockSpec((tokens, count), lambda i: (0, 0)),
-            pl.BlockSpec((3 * count, tile), lambda i: (0, i)),
+            pl.BlockSpec((2 * count, tile), lambda i: (0, i)),
         ],
         out_specs=pl.BlockSpec((tokens, tile), lambda i: (0, i)),
         out_shape=jax.ShapeDtypeStruct((tokens, rows), jnp.bfloat16),
-        compiler_params=pltpu.CompilerParams(vmem_limit_bytes=24 * 1024 * 1024),
+        compiler_params=pltpu.CompilerParams(vmem_limit_bytes=8 * 1024 * 1024),
         cost_estimate=pl.CostEstimate(
-            flops=8 * tokens * rows * count, bytes_accessed=rows * count * 6, transcendentals=0
+            flops=8 * tokens * rows * count, bytes_accessed=rows * count * 4, transcendentals=0
         ),
         name="combine",
     )(product, lead, panel_inputs, aux)
 
 
+def streaming(weight_ref, ring, ring_sems):
+    slots, chunk, width = ring.shape
+    skipped = weight_ref.shape[1] - width
+    total = weight_ref.shape[0] // chunk
+
+    def copy(index, slot):
+        rows = pl.ds(pl.multiple_of(index * chunk, chunk), chunk)
+        return pltpu.make_async_copy(
+            weight_ref.at[rows, pl.ds(skipped, width)], ring.at[slot], ring_sems.at[slot]
+        )
+
+    def run(inputs, use):
+        def step(index, _):
+            slot = lax.rem(index, slots)
+            copy(index, slot).wait()
+            use(pl.ds(pl.multiple_of(index * chunk, chunk), chunk), nt_dot(inputs, ring[slot]))
+
+            @pl.when(index + slots < total)
+            def _():
+                copy(index + slots, slot).start()
+
+            return 0
+
+        lax.fori_loop(0, total, step, 0)
+
+    def begin():
+        for index in range(slots):
+            copy(index, index).start()
+
+    return begin, run
+
+
+def first_kernel(inputs_ref, weight_ref, product_ref, ring, ring_sems):
+    skipped = weight_ref.shape[1] - ring.shape[2]
+    begin, run = streaming(weight_ref, ring, ring_sems)
+    begin()
+
+    def use(rows, product):
+        product_ref[:, rows] = product
+
+    run(inputs_ref[:, skipped:], use)
+
+
+def ring_shape(rows, width):
+    chunk = min(256, rows // 2)
+    return min(6, rows // chunk), chunk, width
+
+
+def first_product(inputs, weight):
+    tokens, features = inputs.shape
+    rows = weight.shape[0]
+    width = features - 2 * BLOCK
+    ring = ring_shape(rows, width)
+    return pl.pallas_call(
+        first_kernel,
+        in_specs=[
+            pl.BlockSpec(memory_space=pltpu.VMEM),
+            pl.BlockSpec(memory_space=pl.ANY),
+        ],
+        out_specs=pl.BlockSpec(memory_space=pltpu.VMEM),
+        out_shape=jax.ShapeDtypeStruct((tokens, rows), jnp.float32),
+        scratch_shapes=[pltpu.VMEM(ring, jnp.bfloat16), pltpu.SemaphoreType.DMA((ring[0],))],
+        compiler_params=pltpu.CompilerParams(vmem_limit_bytes=32 * 1024 * 1024),
+        cost_estimate=pl.CostEstimate(
+            flops=2 * tokens * rows * width, bytes_accessed=rows * width * 2, transcendentals=0
+        ),
+        name="first_product",
+    )(inputs, weight)
+
+
+def turn_kernel(scale, inputs_ref, weight_ref, panel_ref, aux_ref, out_ref, ring, panel, aux,
+                change, ring_sems, side_sems):
+    width = ring.shape[2]
+    skipped = weight_ref.shape[1] - width
+    begin, run = streaming(weight_ref, ring, ring_sems)
+    panel_copy = pltpu.make_async_copy(
+        panel_ref.at[:, pl.ds(skipped, width)], panel, side_sems.at[0]
+    )
+    aux_copy = pltpu.make_async_copy(aux_ref, aux, side_sems.at[1])
+    panel_copy.start()
+    aux_copy.start()
+    begin()
+    panel_copy.wait()
+    panel_inputs = nt_dot(inputs_ref[:, skipped:], panel[...])
+    aux_copy.wait()
+    rows = change.shape[1]
+    tile = min(1024, rows)
+    for at in range(0, rows, tile):
+        place = slice(at, at + tile)
+        change[:, place] = corrected(inputs_ref[:, :skipped], panel_inputs, aux, place)
+
+    def use(place, product):
+        out_ref[:, place] = ((product + change[:, place]) * scale).astype(jnp.bfloat16)
+
+    run(inputs_ref[:, skipped:], use)
+
+
+def turn_product(inputs, weight, panel, aux, scale):
+    tokens, features = inputs.shape
+    rows = weight.shape[0]
+    count = 2 * BLOCK
+    width = features - count
+    ring = ring_shape(rows, width)
+    return pl.pallas_call(
+        functools.partial(turn_kernel, scale),
+        in_specs=[pl.BlockSpec(memory_space=pltpu.VMEM)] + [pl.BlockSpec(memory_space=pl.ANY)] * 3,
+        out_specs=pl.BlockSpec(memory_space=pltpu.VMEM),
+        out_shape=jax.ShapeDtypeStruct((tokens, rows), jnp.bfloat16),
+        scratch_shapes=[
+            pltpu.VMEM(ring, jnp.bfloat16),
+            pltpu.VMEM((count, width), jnp.bfloat16),
+            pltpu.VMEM(aux.shape, jnp.bfloat16),
+            pltpu.VMEM((tokens, rows), jnp.float32),
+            pltpu.SemaphoreType.DMA((ring[0],)),
+            pltpu.SemaphoreType.DMA((2,)),
+        ],
+        compiler_params=pltpu.CompilerParams(vmem_limit_bytes=44 * 1024 * 1024),
+        cost_estimate=pl.CostEstimate(
+            flops=2 * tokens * rows * features, bytes_accessed=rows * width * 2, transcendentals=0
+        ),
+        name="turn_product",
+    )(inputs, weight, panel, aux)
+
+
 def per_device(tokens, up_weight, hess_panel, keep_mask):
     weight = up_weight[0]
     local_panel = hess_panel[0].astype(jnp.bfloat16)
     count = 2 * BLOCK
     features = weight.shape[1]
+    scale = features ** (-0.5)
     row_size = lax.axis_size("row")
     own = tokens.shape[0]
+    held = local_panel.shape[1]
     position = lax.axis_index("layer")
     depth = lax.axis_size("layer")
-
-    width = min(count, local_panel.shape[1])
+    start = lax.axis_index("row") * held
+
+    width = min(count, held)
     share = count // row_size
     factor_share = local_panel[:, :width].reshape(row_size, share * width // count, count)
-    token_share = jnp.broadcast_to(
-        tokens.reshape(1, own * features // count, count), (row_size, own * features // count, count)
-    )
+    cut = own * features // count
+    token_share = jnp.broadcast_to(tokens.reshape(1, cut, count), (row_size, cut, count))
     first = lax.all_to_all(
         jnp.concatenate([token_share, factor_share], 1), "row", split_axis=0, concat_axis=0
     )
-    cut = own * features // count
+    first, local_panel = lax.optimization_barrier((first, local_panel))
     portion = first[:, :cut].reshape(row_size * own, features)
+    full_panel = lax.all_gather(local_panel, "row", axis=1, tiled=True)
+
     owned = [first[o, cut:].reshape(share, width) for o in range(count // width)]
-    factor = gathered(jnp.concatenate(owned, 1), "row").reshape(count, count)
-    full_panel = lax.all_gather(local_panel, "row", axis=1, tiled=True)
-
+    column = lax.broadcasted_iota(jnp.int32, local_panel.shape, 1) + start
+    remote = jnp.where(column < count, jnp.zeros_like(local_panel), local_panel)
+    partial_sum = nt_dot(lax.dynamic_slice_in_dim(portion, start, held, 1), remote)
+    shares = jnp.concatenate([jnp.concatenate(owned, 1), *split_halves(partial_sum)], 0)
+    shares, portion = lax.optimization_barrier((shares, portion))
+    second = gathered(shares, "row")
+    factor = second[:, :share].reshape(count, count)
+    sums = second[:, share:].astype(jnp.float32).reshape(row_size, 2, row_size * own, count)
+
+    product = first_product(portion, weight)
     pruned, aux = eliminate(weight, factor, keep_mask[0])
 
     section_input = tokens
@@ -227,12 +362,9 @@
     for turn in range(depth):
         if turn:
             portion = gathered(section_input, "row").reshape(row_size * own, features)
-        lead = portion[:, :count]
-        column = lax.broadcasted_iota(jnp.int32, portion.shape, 1)
-        rest = jnp.where(column < count, jnp.zeros_like(portion), portion)
-        product = nt_dot(rest, weight)
-        panel_inputs = nt_dot(rest, full_panel)
-        layer_output = combine(product, lead, panel_inputs, aux, features ** (-0.5))
+            layer_output = turn_product(portion, weight, full_panel, aux, scale)
+        else:
+            layer_output = combine(product, portion[:, :count], sums.sum(axis=(0, 1)), aux, scale)
         spread = lax.all_to_all(layer_output, "row", split_axis=0, concat_axis=1, tiled=True)
         hidden = jax.nn.silu(spread.astype(jnp.float32))
         folded = hidden.reshape(own, -1, features).sum(axis=1)

time: 313 us -> 273 us (0.87)
  matrix products: 115 us -> 1.31 us
  Pallas kernels: 27.6 us -> 110 us
  waiting for transfers between devices: 33.4 us -> 11.3 us
  blocking collectives: 66.8 us -> 85.3 us
  starting transfers between devices: 26.1 us -> 18.9 us
  local copies, waits for them, and re-layouts: 17.7 us -> 23.5 us
  other arithmetic: 8.76 us -> 5.1 us
    dot_general x8 -> x1, matrix products: 115 us -> 1.31 us  [nt_dot(): lax.dot_general(left, right, (((1,), (1,)), ((), ())), preferred_element_...]
    pallas_call x0 -> x4, Pallas kernels: none -> 90.5 us  [the longest x3 68.5 us: turn_product(): pl.pallas_call(functools.partial(turn_kernel, scale), in_specs=[pl.BlockS...]
    all_to_all x1 -> x0, waiting for transfers between devices: 21.9 us -> none  [per_device(): lax.all_to_all(jnp.concatenate([token_share, factor_share], 1), 'row', sp...]
    all_to_all x0 -> x1, blocking collectives: none -> 18.7 us  [per_device(): lax.all_to_all(jnp.concatenate([token_share, factor_share], 1), 'row', sp...]
    all_to_all x1 -> x0, starting transfers between devices: 6.33 us -> none  [per_device(): lax.all_to_all(jnp.concatenate([token_share, factor_share], 1), 'row', sp...]
    unnamed x11 -> x21, local copies, waits for them, and re-layouts: 11.3 us -> 17.4 us
    pallas_call x4 -> x1, Pallas kernels: 7.31 us -> 1.45 us  [combine(): pl.pallas_call(functools.partial(combine_kernel, scale), grid=(rows // ti...]
  transfers between devices with their start and end apart: 7 -> 6, of which waited for: 5 -> 4; matrix products, arithmetic and copies ran while one was open for 10% -> 2% of each run, Pallas kernels for 7% -> 15%
where the time goes in v2:
time: 273 us; the launch traced here: 270 us
  Pallas kernels  110 us (40%)
  blocking collectives  85.3 us (31%)
  local copies, waits for them, and re-layouts  23.5 us (9%)
  starting transfers between devices  18.9 us (7%)
  between operations  14.5 us (5%)
  waiting for transfers between devices  11.3 us (4%)
  other arithmetic  5.1 us (2%)
    pallas_call x3, Pallas kernels, turn_product(): pl.pallas_call(functools.partial(turn_kernel, scale), in_specs=[pl.BlockS...  68.5 us
    all_to_all x3, blocking collectives, gathered(): return lax.all_to_all(copies, axis, split_axis=0, concat_axis=0)  36.7 us
    all_to_all x3, blocking collectives, per_device(): lax.all_to_all(layer_output, 'row', split_axis=0, concat_axis=1, tiled=True)  30 us
    pallas_call x1, Pallas kernels, first_product(): pl.pallas_call(first_kernel, in_specs=[pl.BlockSpec(memory_space=pltpu.VM...  22 us
    all_to_all x1, blocking collectives, per_device(): lax.all_to_all(jnp.concatenate([token_share, factor_share], 1), 'row', sp...  18.7 us
    pallas_call x1, Pallas kernels, eliminate(): pl.pallas_call(eliminate_kernel, grid=(rows // tile,), in_specs=[smem, sm...  18.3 us
    unnamed x21, local copies, waits for them, and re-layouts  17.4 us
    ppermute x3, starting transfers between devices, passed_along(): return lax.ppermute(array, axis, pairs)  12.1 us
  transfers between devices with their start and end apart: 6, of which 4 were waited for; matrix products, arithmetic and copies ran while one was open for 2% of the time, Pallas kernels for 15%

profile of v2, /device:TPU:0, one launch (start us, length us, event | category | flops | bytes accessed | tf_op | source)
XLA Modules:
  0.0 270.2 jit_solution(14403580449712549060)
XLA Ops:
  7.2 1.3 convert_bitcast_fusion
  8.5 0.8 broadcast_in_dim.27
  9.4 18.7 %all_to_all.77 = bf16[8,96,256]{2,1,0:T(8,128)(2,1)S(1)} all-to-all(bf16[8,96,256]{2,1,0:T(8,128)(2,1)S(1)} %pad_maximum_fusion), channel_id=1, replica_groups=mesh['layer'=4,'row'=8] {'row'}, dimensions={0} | all-to-all | bytes 786432 | tf_op jit(solution)/shard_map/all_to_all | solution.py:340
  28.3 1.3 subtract_convert_fusion
  29.6 0.7 broadcast_in_dim.57
  30.4 3.4 %all-to-all-start.1 = ((bf16[8,64,256]{2,1,0:T(8,128)(2,1)}), bf16[8,64,256]{2,1,0:T(8,128)(2,1)S(1)}, u32[]{:S(2)}, u32[]{:S(2)}) async-start(bf16[8,64,256]{2,1,0:T(8,128)(2,1)} %broadcast_in_dim.57), calls=%async_computation.1 | async-start | bytes 524288 | tf_op jit(solution)/shard_map/all_to_all | solution.py:25
  33.9 22.0 %first_product.1.product_ref = f32[16,4096]{1,0:T(8,128)S(1)} custom-call(bf16[16,8192]{1,0:T(8,128)(2,1)S(1)} %reshape.153.inputs_ref, bf16[4096,8192]{1,0:T(8,128)(2,1)} %bitcast.3.weight_ref), custom_call_target="tpu_custom_call" | custom-call | flops 1040187392 | bytes 65011712 | tf_op jit(solution)/shard_map/first_product/pallas_call | solution.py:251
  55.9 0.4 copy.23
  56.3 0.3 reshape.160
  57.1 0.5 copy.26.inner_ref
  57.7 0.2 select_reduce_fusion
  58.0 2.2 copy-done.7
  60.2 18.3 %eliminate.1 = (bf16[4096,256]{1,0:T(8,128)(2,1)}, bf16[512,4096]{1,0:T(8,128)(2,1)S(1)}) custom-call(f32[4096]{0:T(1024)S(1)} %reshape.154.scalar_ref, f32[256]{0:T(256)S(1)} %div.59.inverse_ref, bf16[16,256,32]{2,1,0:T(8,128)(2,1)S(1)} %copy.26.inner_ref, bf16[128,256]{1,0:T(8,128)(2,1)S(1)} %pad_maximum_fusion.2.cross_ref, ...), custom_call_target="tpu_custom_call" | custom-call | flops 536870912 | bytes 12582912 | tf_op jit(solution)/shard_map/eliminate/pallas_call | solution.py:134
  78.5 1.5 combine.1
  80.0 2.0 copy-done
  82.0 11.6 %all_to_all.78 = bf16[8,2,4096]{2,1,0:T(2,128)(2,1)S(1)} all-to-all(bf16[8,2,4096]{2,1,0:T(2,128)(2,1)S(1)} %all_to_all.57), channel_id=1, replica_groups=mesh['layer'=4,'row'=8] {'row'}, dimensions={0} | all-to-all | bytes 262144 | tf_op jit(solution)/shard_map/all_to_all | solution.py:368
  94.0 0.3 fusion.4
  94.3 0.2 multiply_reduce_fusion.3
  94.6 3.6 %collective-permute-start = (bf16[2,8192]{1,0:T(2,128)(2,1)S(1)}, bf16[2,8192]{1,0:T(2,128)(2,1)S(1)}, u32[]{:S(2)}, u32[]{:S(2)}) collective-permute-start(bf16[2,8192]{1,0:T(2,128)(2,1)S(1)} %multiply_convert_fusion.3), channel_id=1, source_target_pairs={{0,8},{8,16},{16,24},{1,9},{9,17},{17,25},{2,10},{10,18},{18,26},{... | collective-permute-start | bytes 98312 | tf_op jit(solution)/shard_map/ppermute | solution.py:19
  98.2 1.4 collective-permute-done
  99.7 12.2 %all_to_all.79 = bf16[8,2,8192]{2,1,0:T(2,128)(2,1)S(1)} all-to-all(bf16[8,2,8192]{2,1,0:T(2,128)(2,1)S(1)} %broadcast_in_dim.60), channel_id=1, replica_groups=mesh['layer'=4,'row'=8] {'row'}, dimensions={0} | all-to-all | bytes 524288 | tf_op jit(solution)/shard_map/all_to_all | solution.py:25
  112.1 2.2 copy-done.1
  114.3 2.2 copy-done.4
  116.5 22.8 %turn_product.3 = bf16[16,4096]{1,0:T(8,128)(2,1)S(1)} custom-call(bf16[16,8192]{1,0:T(8,128)(2,1)S(1)} %reshape.157.inputs_ref, bf16[4096,8192]{1,0:T(8,128)(2,1)} %bitcast.3.weight_ref, bf16[256,8192]{1,0:T(8,128)(2,1)S(1)} %copy-done.4, bf16[512,4096]{1,0:T(8,128)(2,1)S(1)} %copy-done.1), custom_call_target="tpu_custom_call" | custom-call | flops 1073741824 | bytes 65011712 | tf_op jit(solution)/shard_map/turn_product/pallas_call | solution.py:301
  139.4 9.2 %all_to_all.80 = bf16[8,2,4096]{2,1,0:T(2,128)(2,1)S(1)} all-to-all(bf16[8,2,4096]{2,1,0:T(2,128)(2,1)S(1)} %all_to_all.60), channel_id=1, replica_groups=mesh['layer'=4,'row'=8] {'row'}, dimensions={0} | all-to-all | bytes 262144 | tf_op jit(solution)/shard_map/all_to_all | solution.py:368
  149.0 0.3 fusion.5
  149.3 0.2 multiply_reduce_fusion.2
  149.6 4.2 %collective-permute-start.1 = (bf16[2,8192]{1,0:T(2,128)(2,1)S(1)}, bf16[2,8192]{1,0:T(2,128)(2,1)S(1)}, u32[]{:S(2)}, u32[]{:S(2)}) collective-permute-start(bf16[2,8192]{1,0:T(2,128)(2,1)S(1)} %multiply_convert_fusion.2), channel_id=1, source_target_pairs={{0,8},{8,16},{16,24},{1,9},{9,17},{17,25},{2,10},{10,18},{18,26},{... | collective-permute-start | bytes 98312 | tf_op jit(solution)/shard_map/ppermute | solution.py:19
  153.8 1.6 collective-permute-done.1
  155.5 12.2 %all_to_all.81 = bf16[8,2,8192]{2,1,0:T(2,128)(2,1)S(1)} all-to-all(bf16[8,2,8192]{2,1,0:T(2,128)(2,1)S(1)} %broadcast_in_dim.61), channel_id=1, replica_groups=mesh['layer'=4,'row'=8] {'row'}, dimensions={0} | all-to-all | bytes 524288 | tf_op jit(solution)/shard_map/all_to_all | solution.py:25
  167.9 2.2 copy-done.2
  170.1 2.2 copy-done.5
  172.2 22.8 %turn_product.4 = bf16[16,4096]{1,0:T(8,128)(2,1)S(1)} custom-call(bf16[16,8192]{1,0:T(8,128)(2,1)S(1)} %reshape.158.inputs_ref, bf16[4096,8192]{1,0:T(8,128)(2,1)} %bitcast.3.weight_ref, bf16[256,8192]{1,0:T(8,128)(2,1)S(1)} %copy-done.5, bf16[512,4096]{1,0:T(8,128)(2,1)S(1)} %copy-done.2), custom_call_target="tpu_custom_call" | custom-call | flops 1073741824 | bytes 65011712 | tf_op jit(solution)/shard_map/turn_product/pallas_call | solution.py:301
  195.2 9.2 %all_to_all.82 = bf16[8,2,4096]{2,1,0:T(2,128)(2,1)S(1)} all-to-all(bf16[8,2,4096]{2,1,0:T(2,128)(2,1)S(1)} %all_to_all.63), channel_id=1, replica_groups=mesh['layer'=4,'row'=8] {'row'}, dimensions={0} | all-to-all | bytes 262144 | tf_op jit(solution)/shard_map/all_to_all | solution.py:368
  204.8 0.3 fusion.6
  205.0 0.2 multiply_reduce_fusion.1
  205.3 4.3 %collective-permute-start.2 = (bf16[2,8192]{1,0:T(2,128)(2,1)S(1)}, bf16[2,8192]{1,0:T(2,128)(2,1)S(1)}, u32[]{:S(2)}, u32[]{:S(2)}) collective-permute-start(bf16[2,8192]{1,0:T(2,128)(2,1)S(1)} %multiply_convert_fusion.1), channel_id=1, source_target_pairs={{0,8},{8,16},{16,24},{1,9},{9,17},{17,25},{2,10},{10,18},{18,26},{... | collective-permute-start | bytes 98312 | tf_op jit(solution)/shard_map/ppermute | solution.py:19
  209.6 1.6 collective-permute-done.2
  211.4 12.2 %all_to_all.83 = bf16[8,2,8192]{2,1,0:T(2,128)(2,1)S(1)} all-to-all(bf16[8,2,8192]{2,1,0:T(2,128)(2,1)S(1)} %broadcast_in_dim.62), channel_id=1, replica_groups=mesh['layer'=4,'row'=8] {'row'}, dimensions={0} | all-to-all | bytes 524288 | tf_op jit(solution)/shard_map/all_to_all | solution.py:25
  223.7 2.2 copy-done.3
  225.9 2.2 copy-done.6
  228.1 22.8 %turn_product.5 = bf16[16,4096]{1,0:T(8,128)(2,1)S(1)} custom-call(bf16[16,8192]{1,0:T(8,128)(2,1)S(1)} %reshape.159.inputs_ref, bf16[4096,8192]{1,0:T(8,128)(2,1)} %bitcast.3.weight_ref, bf16[256,8192]{1,0:T(8,128)(2,1)S(1)} %copy-done.6, bf16[512,4096]{1,0:T(8,128)(2,1)S(1)} %copy-done.3), custom_call_target="tpu_custom_call" | custom-call | flops 1073741824 | bytes 65011712 | tf_op jit(solution)/shard_map/turn_product/pallas_call | solution.py:301
  250.9 0.7 all_to_all.66
  251.6 3.4 %all-to-all-start.8 = ((bf16[8,2,4096]{2,1,0:T(2,128)(2,1)}), bf16[8,2,4096]{2,1,0:T(2,128)(2,1)S(1)}, u32[]{:S(2)}, u32[]{:S(2)}) async-start(bf16[8,2,4096]{2,1,0:T(2,128)(2,1)} %all_to_all.66), calls=%async_computation.8 | async-start | bytes 262144 | tf_op jit(solution)/shard_map/all_to_all | solution.py:368
  255.0 6.7 %all-to-all-done.8 = bf16[8,2,4096]{2,1,0:T(2,128)(2,1)S(1)} async-done(((bf16[8,2,4096]{2,1,0:T(2,128)(2,1)}), bf16[8,2,4096]{2,1,0:T(2,128)(2,1)S(1)}, u32[]{:S(2)}, u32[]{:S(2)}) %all-to-all-start.8) | async-done | bytes 131104 | tf_op jit(solution)/shard_map/all_to_all | solution.py:368
  262.1 0.3 fusion.7
  262.4 0.2 multiply_reduce_fusion
  262.6 0.7 fusion.8
  (69 shorter events, 3.8 us)
Async XLA Ops:
  7.2 104.9 %all-gather.2.cloned.1.call-start = ((), (), s32[]{:S(2)}) async-start(), calls=%async_computation.9 | async-start | bytes 4718592 | tf_op jit(solution)/shard_map/all_gather | solution.py:345
  8.5 19.6 %copy-start.8 = (bf16[256,1024]{1,0:T(8,128)(2,1)}, bf16[256,1024]{1,0:T(8,128)(2,1)S(1)}, u32[]{:S(2)}) copy-start(bf16[256,1024]{1,0:T(8,128)(2,1)S(1)} %convert_bitcast_fusion) | copy-start | bytes 1572868
  30.4 25.5 %all-to-all-start.1 = ((bf16[8,64,256]{2,1,0:T(8,128)(2,1)}), bf16[8,64,256]{2,1,0:T(8,128)(2,1)S(1)}, u32[]{:S(2)}, u32[]{:S(2)}) async-start(bf16[8,64,256]{2,1,0:T(8,128)(2,1)} %broadcast_in_dim.57), calls=%async_computation.1 | async-start | bytes 524288 | tf_op jit(solution)/shard_map/all_to_all | solution.py:25
  58.0 2.2 copy-start.7
  78.5 15.8 %copy-start.9 = (bf16[2,8192]{1,0:T(2,128)(2,1)S(1)}, bf16[2,8192]{1,0:T(2,128)(2,1)}, u32[]{:S(2)}) copy-start(bf16[2,8192]{1,0:T(2,128)(2,1)} %param.4) | copy-start | bytes 98308
  79.9 2.0 copy-start
  94.6 5.0 %collective-permute-start = (bf16[2,8192]{1,0:T(2,128)(2,1)S(1)}, bf16[2,8192]{1,0:T(2,128)(2,1)S(1)}, u32[]{:S(2)}, u32[]{:S(2)}) collective-permute-start(bf16[2,8192]{1,0:T(2,128)(2,1)S(1)} %multiply_convert_fusion.3), channel_id=1, source_target_pairs={{0,8},{8,16},{16,24},{1,9},{9,17},{17,25},{2,10},{10,18},{18,26},{... | collective-permute-start | bytes 98312 | tf_op jit(solution)/shard_map/ppermute | solution.py:19
  112.1 2.2 copy-start.1
  114.3 2.2 copy-start.4
  149.6 5.8 %collective-permute-start.1 = (bf16[2,8192]{1,0:T(2,128)(2,1)S(1)}, bf16[2,8192]{1,0:T(2,128)(2,1)S(1)}, u32[]{:S(2)}, u32[]{:S(2)}) collective-permute-start(bf16[2,8192]{1,0:T(2,128)(2,1)S(1)} %multiply_convert_fusion.2), channel_id=1, source_target_pairs={{0,8},{8,16},{16,24},{1,9},{9,17},{17,25},{2,10},{10,18},{18,26},{... | collective-permute-start | bytes 98312 | tf_op jit(solution)/shard_map/ppermute | solution.py:19
  167.9 2.2 copy-start.2
  170.0 2.2 copy-start.5
  205.3 5.9 %collective-permute-start.2 = (bf16[2,8192]{1,0:T(2,128)(2,1)S(1)}, bf16[2,8192]{1,0:T(2,128)(2,1)S(1)}, u32[]{:S(2)}, u32[]{:S(2)}) collective-permute-start(bf16[2,8192]{1,0:T(2,128)(2,1)S(1)} %multiply_convert_fusion.1), channel_id=1, source_target_pairs={{0,8},{8,16},{16,24},{1,9},{9,17},{17,25},{2,10},{10,18},{18,26},{... | collective-permute-start | bytes 98312 | tf_op jit(solution)/shard_map/ppermute | solution.py:19
  223.7 2.2 copy-start.3
  225.9 2.2 copy-start.6
  251.6 10.1 %all-to-all-start.8 = ((bf16[8,2,4096]{2,1,0:T(2,128)(2,1)}), bf16[8,2,4096]{2,1,0:T(2,128)(2,1)S(1)}, u32[]{:S(2)}, u32[]{:S(2)}) async-start(bf16[8,2,4096]{2,1,0:T(2,128)(2,1)} %all_to_all.66), calls=%async_computation.8 | async-start | bytes 262144 | tf_op jit(solution)/shard_map/all_to_all | solution.py:368
Sparse Core Ops, SparseCore 0:
  28.2 50.8 all-gather.1

commit v3 on v2

--- a/solution.py
+++ b/solution.py
@@ -9,14 +9,11 @@
 
 BLOCK = 128
 SUB = 16
+HELD = 7
+ELIMINATE_VMEM = 56 * 1024 * 1024
+TURN_VMEM = 32 * 1024 * 1024
 
 epsilon = 1e-05
-
-
-def passed_along(array, axis, by):
-    size = lax.axis_size(axis)
-    pairs = [(i, i + by) for i in range(size) if 0 <= i + by < size]
-    return lax.ppermute(array, axis, pairs)
 
 
 def gathered(array, axis):
@@ -151,7 +148,7 @@
             jax.ShapeDtypeStruct((2 * count, rows), jnp.bfloat16),
         ],
         scratch_shapes=[pltpu.VMEM((tile * count // 128, 128), jnp.float32)] * 3,
-        compiler_params=pltpu.CompilerParams(vmem_limit_bytes=26 * 1024 * 1024),
+        compiler_params=pltpu.CompilerParams(vmem_limit_bytes=ELIMINATE_VMEM),
         cost_estimate=pl.CostEstimate(
             flops=2 * rows * count * count, bytes_accessed=rows * count * 12, transcendentals=0
         ),
@@ -167,32 +164,79 @@
     return nn_dot(lead, aux_ref[0:count, place]) - both[:tokens] - both[tokens:]
 
 
-def combine_kernel(scale, product_ref, lead_ref, panel_ref, aux_ref, out_ref):
-    change = corrected(lead_ref[...], panel_ref[...], aux_ref, slice(None))
-    out_ref[...] = ((product_ref[...] + change) * scale).astype(jnp.bfloat16)
-
-
-def combine(product, lead, panel_inputs, aux, scale):
+def hand_out(out_ref, value, inputs, where_ref, place, scale):
+    units = (value * scale).astype(jnp.bfloat16).astype(jnp.float32)
+    units = units / (1.0 + jnp.exp(-units))
+    first, size = place
+    at = pl.ds(pl.multiple_of(where_ref[0] + first, 128), size)
+    units = units + inputs[:, at].astype(jnp.float32) * where_ref[1].astype(jnp.float32)
+    copies, own, _ = out_ref.shape
+    peers = value.shape[0] // own
+    for peer in range(peers):
+        piece = units[peer * own : (peer + 1) * own].astype(jnp.bfloat16)
+        for copy in range(peer, copies, peers):
+            out_ref[copy, :, pl.ds(first, size)] = piece
+
+
+def combine_kernel(scale, where_ref, product_ref, inputs_ref, panel_ref, aux_ref, out_ref):
+    count = 2 * BLOCK
+    rows = product_ref.shape[1]
+    tile = min(1024, rows)
+    for first in range(0, rows, tile):
+        place = slice(first, first + tile)
+        change = corrected(inputs_ref[:, :count], panel_ref[...], aux_ref, place)
+        value = product_ref[:, place] + change
+        hand_out(out_ref, value, inputs_ref, where_ref, (first, tile), scale)
+
+
+def combine(where, product, inputs, panel_inputs, aux, scale, out_shape):
     tokens, rows = product.shape
     count = 2 * BLOCK
-    tile = min(1024, rows)
     return pl.pallas_call(
         functools.partial(combine_kernel, scale),
-        grid=(rows // tile,),
-        in_specs=[
-            pl.BlockSpec((tokens, tile), lambda i: (0, i)),
-            pl.BlockSpec((tokens, count), lambda i: (0, 0)),
-            pl.BlockSpec((tokens, count), lambda i: (0, 0)),
-            pl.BlockSpec((2 * count, tile), lambda i: (0, i)),
-        ],
-        out_specs=pl.BlockSpec((tokens, tile), lambda i: (0, i)),
-        out_shape=jax.ShapeDtypeStruct((tokens, rows), jnp.bfloat16),
-        compiler_params=pltpu.CompilerParams(vmem_limit_bytes=8 * 1024 * 1024),
+        in_specs=[pl.BlockSpec(memory_space=pltpu.SMEM)] + [pl.BlockSpec(memory_space=pltpu.VMEM)] * 4,
+        out_specs=pl.BlockSpec(memory_space=pltpu.VMEM),
+        out_shape=out_shape,
+        compiler_params=pltpu.CompilerParams(vmem_limit_bytes=16 * 1024 * 1024),
         cost_estimate=pl.CostEstimate(
             flops=8 * tokens * rows * count, bytes_accessed=rows * count * 4, transcendentals=0
         ),
         name="combine",
-    )(product, lead, panel_inputs, aux)
+    )(where, product, inputs, panel_inputs, aux)
+
+
+def fold_kernel(spread_ref, copies_ref, produced_ref):
+    peers, own, features = copies_ref.shape
+    rows = spread_ref.shape[2]
+    parts = []
+    for first in range(0, features, rows):
+        part = None
+        for peer in range(peers):
+            if peer * rows % features == first:
+                units = spread_ref[peer].astype(jnp.float32)
+                part = units if part is None else part + units
+        parts.append(part)
+    combined = jnp.concatenate(parts, 1)
+    moment = jnp.sum(combined * combined, axis=1, keepdims=True) * (1.0 / features)
+    produced = (combined * lax.rsqrt(moment + epsilon)).astype(jnp.bfloat16)
+    produced_ref[...] = produced
+    for peer in range(peers):
+        copies_ref[peer] = produced
+
+
+def fold(spread, peers, features):
+    own = spread.shape[1]
+    return pl.pallas_call(
+        fold_kernel,
+        in_specs=[pl.BlockSpec(memory_space=pltpu.VMEM)],
+        out_specs=[pl.BlockSpec(memory_space=pltpu.VMEM)] * 2,
+        out_shape=[
+            jax.ShapeDtypeStruct((peers, own, features), jnp.bfloat16),
+            jax.ShapeDtypeStruct((own, features), jnp.bfloat16),
+        ],
+        compiler_params=pltpu.CompilerParams(vmem_limit_bytes=8 * 1024 * 1024),
+        name="fold",
+    )(spread)
 
 
 def streaming(weight_ref, ring, ring_sems):
@@ -265,58 +309,138 @@
     )(inputs, weight)
 
 
-def turn_kernel(scale, inputs_ref, weight_ref, panel_ref, aux_ref, out_ref, ring, panel, aux,
-                change, ring_sems, side_sems):
-    width = ring.shape[2]
+def turn_kernel(scale, held_count, fill, where_ref, gathered_ref, weight_ref, panel_ref, aux_ref,
+                *rest):
+    if fill:
+        out_ref, held_ref, held_sems = rest[0], rest[1], rest[-1]
+        rest = rest[:-1]
+    else:
+        held_ref, out_ref = rest[0], rest[1 if held_count else 0]
+    ring, panel, aux, wide, inputs, product, ring_sems, side_sems = rest[-8:]
+    slots, chunk, width = ring.shape
     skipped = weight_ref.shape[1] - width
-    begin, run = streaming(weight_ref, ring, ring_sems)
+    streams = weight_ref.shape[0] // chunk - held_count
+    ahead = min(2, held_count)
+
+    def copy(index, slot):
+        rows = pl.ds(pl.multiple_of((held_count + index) * chunk, chunk), chunk)
+        return pltpu.make_async_copy(
+            weight_ref.at[rows, pl.ds(skipped, width)], ring.at[slot], ring_sems.at[slot]
+        )
+
     panel_copy = pltpu.make_async_copy(
         panel_ref.at[:, pl.ds(skipped, width)], panel, side_sems.at[0]
     )
     aux_copy = pltpu.make_async_copy(aux_ref, aux, side_sems.at[1])
+    def held_copy(index):
+        rows = pl.ds(pl.multiple_of(index * chunk, chunk), chunk)
+        return pltpu.make_async_copy(
+            weight_ref.at[rows, pl.ds(skipped, width)], held_ref.at[rows, :], held_sems.at[index]
+        )
+
+    if fill:
+        for index in range(ahead):
+            held_copy(index).start()
     panel_copy.start()
     aux_copy.start()
-    begin()
+    for index in range(slots):
+        copy(index, index).start()
+    if fill:
+        for index in range(ahead, held_count):
+            held_copy(index).start()
+
+    peers, own, _ = gathered_ref.shape
+    for peer in range(peers):
+        wide[peer * own : (peer + 1) * own, :] = gathered_ref[peer].astype(jnp.float32)
+    inputs[...] = wide[...].astype(jnp.bfloat16)
+
+    def place_of(index):
+        return pl.multiple_of(index * chunk, chunk)
+
+    def held_product(index):
+        if fill:
+            held_copy(index).wait()
+        return nt_dot(inputs[:, skipped:], held_ref[pl.ds(place_of(index), chunk), :])
+
+    for index in range(ahead):
+        product[:, index * chunk : (index + 1) * chunk] = held_product(index)
     panel_copy.wait()
-    panel_inputs = nt_dot(inputs_ref[:, skipped:], panel[...])
+    panel_inputs = nt_dot(inputs[:, skipped:], panel[...])
     aux_copy.wait()
-    rows = change.shape[1]
+    rows = product.shape[1]
     tile = min(1024, rows)
-    for at in range(0, rows, tile):
-        place = slice(at, at + tile)
-        change[:, place] = corrected(inputs_ref[:, :skipped], panel_inputs, aux, place)
-
-    def use(place, product):
-        out_ref[:, place] = ((product + change[:, place]) * scale).astype(jnp.bfloat16)
-
-    run(inputs_ref[:, skipped:], use)
-
-
-def turn_product(inputs, weight, panel, aux, scale):
-    tokens, features = inputs.shape
+    early = ahead * chunk
+    for first in range(0, rows, tile):
+        change = corrected(inputs[:, :skipped], panel_inputs, aux, slice(first, first + tile))
+        both = min(max(early - first, 0), tile)
+        if both:
+            product[:, first : first + both] += change[:, :both]
+        if both < tile:
+            product[:, first + both : first + tile] = change[:, both:]
+
+    def use(index, value):
+        first = place_of(index)
+        value = product[:, pl.ds(first, chunk)] + value
+        hand_out(out_ref, value, inputs, where_ref, (first, chunk), scale)
+
+    for index in range(ahead):
+        value = product[:, index * chunk : (index + 1) * chunk]
+        hand_out(out_ref, value, inputs, where_ref, (index * chunk, chunk), scale)
+
+    def step(index, _):
+        if held_count > ahead:
+            @pl.when(index + ahead < held_count)
+            def _():
+                use(index + ahead, held_product(index + ahead))
+
+        slot = lax.rem(index, slots)
+        copy(index, slot).wait()
+        use(held_count + index, nt_dot(inputs[:, skipped:], ring[slot]))
+
+        @pl.when(index + slots < streams)
+        def _():
+            copy(index + slots, slot).start()
+
+        return 0
+
+    lax.fori_loop(0, streams, step, 0)
+
+
+def turn_product(where, gathered_inputs, weight, panel, aux, held, held_count, scale, out_shape):
+    peers, own, features = gathered_inputs.shape
+    tokens = peers * own
     rows = weight.shape[0]
     count = 2 * BLOCK
     width = features - count
-    ring = ring_shape(rows, width)
+    chunk = min(256, rows // 2)
+    fill = held is None and held_count > 0
+    ring = (min(3 if held_count else 6, rows // chunk - held_count), chunk, width)
+    vmem = pl.BlockSpec(memory_space=pltpu.VMEM)
+    hbm = pl.BlockSpec(memory_space=pl.ANY)
+    operands = [where, gathered_inputs, weight, panel, aux]
+    if held is not None:
+        operands.append(pltpu.with_memory_space_constraint(held, pltpu.VMEM))
     return pl.pallas_call(
-        functools.partial(turn_kernel, scale),
-        in_specs=[pl.BlockSpec(memory_space=pltpu.VMEM)] + [pl.BlockSpec(memory_space=pl.ANY)] * 3,
-        out_specs=pl.BlockSpec(memory_space=pltpu.VMEM),
-        out_shape=jax.ShapeDtypeStruct((tokens, rows), jnp.bfloat16),
+        functools.partial(turn_kernel, scale, held_count, fill),
+        in_specs=[pl.BlockSpec(memory_space=pltpu.SMEM), vmem, hbm, hbm, hbm] + [vmem] * (len(operands) - 5),
+        out_specs=[vmem] * 2 if fill else vmem,
+        out_shape=[out_shape, pltpu.VMEM((held_count * chunk, width), jnp.bfloat16)] if fill else out_shape,
         scratch_shapes=[
             pltpu.VMEM(ring, jnp.bfloat16),
             pltpu.VMEM((count, width), jnp.bfloat16),
             pltpu.VMEM(aux.shape, jnp.bfloat16),
+            pltpu.VMEM((tokens, features), jnp.float32),
+            pltpu.VMEM((tokens, features), jnp.bfloat16),
             pltpu.VMEM((tokens, rows), jnp.float32),
             pltpu.SemaphoreType.DMA((ring[0],)),
             pltpu.SemaphoreType.DMA((2,)),
-        ],
-        compiler_params=pltpu.CompilerParams(vmem_limit_bytes=44 * 1024 * 1024),
+        ] + [pltpu.SemaphoreType.DMA((held_count,))] * fill,
+        compiler_params=pltpu.CompilerParams(vmem_limit_bytes=TURN_VMEM),
         cost_estimate=pl.CostEstimate(
             flops=2 * tokens * rows * features, bytes_accessed=rows * width * 2, transcendentals=0
         ),
         name="turn_product",
-    )(inputs, weight, panel, aux)
+    )(*operands)
 
 
 def per_device(tokens, up_weight, hess_panel, keep_mask):
@@ -357,23 +481,39 @@
     product = first_product(portion, weight)
     pruned, aux = eliminate(weight, factor, keep_mask[0])
 
-    section_input = tokens
+    rows = weight.shape[0]
+    from_row = lax.axis_index("row") * rows
+    where = jnp.stack([from_row % features, (from_row < features).astype(jnp.int32)])
+    held_count = rows // min(256, rows // 2) * HELD // 16
+    held = None
     results = jnp.zeros_like(tokens)
     for turn in range(depth):
+        last = turn + 1 == depth
+        out_shape = jax.ShapeDtypeStruct(((1 if last else 2) * row_size, own, rows), jnp.bfloat16)
         if turn:
-            portion = gathered(section_input, "row").reshape(row_size * own, features)
-            layer_output = turn_product(portion, weight, full_panel, aux, scale)
+            units = turn_product(
+                where, copies, weight, full_panel, aux, held, held_count, scale, out_shape
+            )
+            if held_count and held is None:
+                units, held = units
         else:
-            layer_output = combine(product, portion[:, :count], sums.sum(axis=(0, 1)), aux, scale)
-        spread = lax.all_to_all(layer_output, "row", split_axis=0, concat_axis=1, tiled=True)
-        hidden = jax.nn.silu(spread.astype(jnp.float32))
-        folded = hidden.reshape(own, -1, features).sum(axis=1)
-        combined = section_input.astype(jnp.float32) + folded
-        moment = jnp.mean(combined * combined, axis=-1, keepdims=True)
-        produced = (combined * lax.rsqrt(moment + epsilon)).astype(jnp.bfloat16)
+            units = combine(where, product, portion, sums.sum(axis=(0, 1)), aux, scale, out_shape)
+        if last:
+            spread = lax.all_to_all(units, "row", split_axis=0, concat_axis=0)
+        else:
+            pair = [turn, turn + 1]
+            others = [layer for layer in range(depth) if layer not in pair]
+            groups = [
+                [layer * row_size + peer for layer in layers for peer in range(row_size)]
+                for layers in [pair] + [others[i : i + 2] for i in range(0, len(others), 2)]
+            ]
+            spread = lax.all_to_all(
+                units, ("layer", "row"), split_axis=0, concat_axis=0, axis_index_groups=groups
+            )
+        copies, produced = fold(spread, row_size, features)
         results = jnp.where(position == turn, produced, results)
-        if turn + 1 < depth:
-            section_input = passed_along(produced, "layer", 1)
+        if not last:
+            copies = lax.all_to_all(copies, "row", split_axis=0, concat_axis=0)
     return (results[None], pruned[None])
 
 

time: 273 us -> 271 us (level)
  Pallas kernels: 110 us -> 129 us
  local copies, waits for them, and re-layouts: 23.5 us -> 7.62 us
  blocking collectives: 85.3 us -> 101 us
  starting transfers between devices: 18.9 us -> 6.83 us
  waiting for transfers between devices: 11.3 us -> 6.72 us
    pallas_call x4 -> x8, Pallas kernels: 69.9 us -> 87.2 us  [the longest x3 84.3 us: turn_product(): pl.pallas_call(functools.partial(turn_kernel, scale, held_count, fill), i...]
    all_to_all x6, blocking collectives: 66.6 us -> 82.4 us  [the longest x3 44 us: per_device(): lax.all_to_all(units, ('layer', 'row'), split_axis=0, concat_axis=0, axis...]
    unnamed x21 -> x7, local copies, waits for them, and re-layouts: 17.4 us -> 2.3 us
    ppermute x3 -> x0, starting transfers between devices: 12.1 us -> none  [passed_along(): return lax.ppermute(array, axis, pairs)]
    ppermute x3 -> x0, waiting for transfers between devices: 4.55 us -> none  [passed_along(): return lax.ppermute(array, axis, pairs)]
  transfers between devices with their start and end apart: 6 -> 3, of which waited for: 4 -> 1; matrix products, arithmetic and copies ran while one was open for 2% -> 3% of each run, Pallas kernels for 15% -> 16%
where the time goes in v3:
time: 271 us; the launch traced here: 270 us
  Pallas kernels  129 us (48%)
  blocking collectives  101 us (37%)
  between operations  14.3 us (5%)
  local copies, waits for them, and re-layouts  7.62 us (3%)
  starting transfers between devices  6.83 us (3%)
  waiting for transfers between devices  6.72 us (2%)
  other arithmetic  3.17 us (1%)
    pallas_call x3, Pallas kernels, turn_product(): pl.pallas_call(functools.partial(turn_kernel, scale, held_count, fill), i...  84.3 us
    all_to_all x3, blocking collectives, per_device(): lax.all_to_all(units, ('layer', 'row'), split_axis=0, concat_axis=0, axis...  44 us
    all_to_all x3, blocking collectives, per_device(): copies = lax.all_to_all(copies, 'row', split_axis=0, concat_axis=0)  38.4 us
    pallas_call x1, Pallas kernels, first_product(): pl.pallas_call(first_kernel, in_specs=[pl.BlockSpec(memory_space=pltpu.VM...  22 us
    pallas_call x1, Pallas kernels, eliminate(): pl.pallas_call(eliminate_kernel, grid=(rows // tile,), in_specs=[smem, sm...  19.7 us
    all_to_all x1, blocking collectives, per_device(): lax.all_to_all(jnp.concatenate([token_share, factor_share], 1), 'row', sp...  18.7 us
    all_to_all x1, waiting for transfers between devices, per_device(): spread = lax.all_to_all(units, 'row', split_axis=0, concat_axis=0)  6.7 us
  transfers between devices with their start and end apart: 3, of which 1 were waited for; matrix products, arithmetic and copies ran while one was open for 3% of the time, Pallas kernels for 16%

profile of v3, /device:TPU:0, one launch (start us, length us, event | category | flops | bytes accessed | tf_op | source)
XLA Modules:
  0.0 269.9 jit_solution(14586638133891017001)
XLA Ops:
  7.2 0.0 all-gather.2.cloned.1.call-start
  7.2 1.3 convert_bitcast_fusion
  8.5 0.0 copy-start.2
  8.5 0.8 broadcast_in_dim.32
  9.4 18.7 %all_to_all.45 = bf16[8,96,256]{2,1,0:T(8,128)(2,1)S(1)} all-to-all(bf16[8,96,256]{2,1,0:T(8,128)(2,1)S(1)} %pad_maximum_fusion), channel_id=1, replica_groups=mesh['layer'=4,'row'=8] {'row'}, dimensions={0} | all-to-all | bytes 786432 | tf_op jit(solution)/shard_map/all_to_all | solution.py:464
  28.1 0.0 copy-done.2
  28.1 0.0 all-gather.2.cloned.1.call-update
  28.2 0.1 reshape.81.inputs_ref
  28.4 1.3 subtract_convert_fusion
  29.7 0.7 broadcast_in_dim.35
  30.4 3.4 %all-to-all-start.1 = ((bf16[8,64,256]{2,1,0:T(8,128)(2,1)}), bf16[8,64,256]{2,1,0:T(8,128)(2,1)S(1)}, u32[]{:S(2)}, u32[]{:S(2)}) async-start(bf16[8,64,256]{2,1,0:T(8,128)(2,1)} %broadcast_in_dim.35), calls=%async_computation.1 | async-start | bytes 524288 | tf_op jit(solution)/shard_map/all_to_all | solution.py:22
  33.8 0.1 pad_add_fusion.where_ref
  33.9 0.0 copy-start.1
  33.9 22.0 %first_product.1.product_ref = f32[16,4096]{1,0:T(8,128)S(1)} custom-call(bf16[16,8192]{1,0:T(8,128)(2,1)S(1)} %reshape.81.inputs_ref, bf16[4096,8192]{1,0:T(8,128)(2,1)} %bitcast.5.weight_ref), custom_call_target="tpu_custom_call" | custom-call | flops 1040187392 | bytes 65011712 | tf_op jit(solution)/shard_map/first_product/pallas_call | solution.py:295
  55.9 0.0 all-to-all-done.1
  56.0 0.4 copy.15
  56.4 0.3 reshape.86
  56.7 0.2 select_reduce_fusion.1
  56.9 0.1 copy.16
  57.0 0.7 reshape.82.scalar_ref
  57.7 1.4 copy.18.inner_ref
  59.1 0.1 copy.19
  59.2 0.2 select_reduce_fusion
  59.4 0.7 div.30.inverse_ref
  60.1 0.6 pad_maximum_fusion.2.cross_ref
  60.7 19.7 %eliminate.1 = (bf16[4096,256]{1,0:T(8,128)(2,1)}, bf16[512,4096]{1,0:T(8,128)(2,1)}) custom-call(f32[4096]{0:T(1024)} %reshape.82.scalar_ref, f32[256]{0:T(256)} %div.30.inverse_ref, bf16[16,256,32]{2,1,0:T(8,128)(2,1)} %copy.18.inner_ref, bf16[128,256]{1,0:T(8,128)(2,1)} %pad_maximum_fusion.2.cross_ref, bf16[4096,8192]{1,0:T(8,128)(2,1)} %bitcast.5.weight_ref, ...), custom_call_target="tpu_custom_call" | custom-call | flops 536870912 | bytes 12582912 | tf_op jit(solution)/shard_map/eliminate/pallas_call | solution.py:131
  80.4 0.0 copy-done.1
  80.4 0.0 copy-start
  80.4 2.2 copy-done
  82.6 1.3 combine.1
  83.9 15.9 %all_to_all.46.spread_ref = bf16[16,2,4096]{2,1,0:T(2,128)(2,1)S(1)} all-to-all(bf16[16,2,4096]{2,1,0:T(2,128)(2,1)S(1)} %combine.1), channel_id=1, replica_groups={{0,1,2,3,4,5,6,7,8,9,10,11,12,13,14,15},{16,17,18,19,20,21,22,23,24,25,..., dimensions={0} | all-to-all | bytes 524288 | tf_op jit(solution)/shard_map/all_to_all | solution.py:510
  99.8 0.2 fold.4
  100.0 12.8 %all_to_all.47.gathered_ref = bf16[8,2,8192]{2,1,0:T(2,128)(2,1)} all-to-all(bf16[8,2,8192]{2,1,0:T(2,128)(2,1)S(1)} %get-tuple-element.22), channel_id=1, replica_groups=mesh['layer'=4,'row'=8] {'row'}, dimensions={0} | all-to-all | bytes 524288 | tf_op jit(solution)/shard_map/all_to_all | solution.py:516
  112.8 0.0 all-gather.2.cloned.1.call-done.panel_ref
  112.8 32.9 %turn_product.3 = (bf16[16,2,4096]{2,1,0:T(2,128)(2,1)}, bf16[1792,7936]{1,0:T(8,128)(2,1)S(1)}) custom-call(s32[2]{0:T(128)} %copy-done.1, bf16[8,2,8192]{2,1,0:T(2,128)(2,1)} %all_to_all.47.gathered_ref, bf16[4096,8192]{1,0:T(8,128)(2,1)} %bitcast.5.weight_ref, bf16[256,8192]{1,0:T(8,128)(2,1)} %all-gather.2.cloned.1.call-done.panel_ref, ...), custom_call_target="tpu_custom_call" | custom-call | flops 1073741824 | bytes 65011712 | tf_op jit(solution)/shard_map/turn_product/pallas_call | solution.py:423
  145.7 14.5 %all_to_all.48.spread_ref = bf16[16,2,4096]{2,1,0:T(2,128)(2,1)S(1)} all-to-all(bf16[16,2,4096]{2,1,0:T(2,128)(2,1)} %get-tuple-element.23), channel_id=1, replica_groups={{8,9,10,11,12,13,14,15,16,17,18,19,20,21,22,23},{0,1,2,3,4,5,6,7,24,25,..., dimensions={0} | all-to-all | bytes 524288 | tf_op jit(solution)/shard_map/all_to_all | solution.py:510
  160.3 0.2 fold.5
  160.5 12.8 %all_to_all.49.gathered_ref = bf16[8,2,8192]{2,1,0:T(2,128)(2,1)} all-to-all(bf16[8,2,8192]{2,1,0:T(2,128)(2,1)S(1)} %get-tuple-element.24), channel_id=1, replica_groups=mesh['layer'=4,'row'=8] {'row'}, dimensions={0} | all-to-all | bytes 524288 | tf_op jit(solution)/shard_map/all_to_all | solution.py:516
  173.3 25.8 %turn_product.4 = bf16[16,2,4096]{2,1,0:T(2,128)(2,1)} custom-call(s32[2]{0:T(128)} %copy-done.1, bf16[8,2,8192]{2,1,0:T(2,128)(2,1)} %all_to_all.49.gathered_ref, bf16[4096,8192]{1,0:T(8,128)(2,1)} %bitcast.5.weight_ref, bf16[256,8192]{1,0:T(8,128)(2,1)} %all-gather.2.cloned.1.call-done.panel_ref, bf16[512,4096]{1,0:T(8,128)(2,1)} %get-tuple-element.21.aux_ref, ...), custom_call_target="tpu_custom_call" | custom-call | flops 1073741824 | bytes 65011712 | tf_op jit(solution)/shard_map/turn_product/pallas_call | solution.py:423
  199.1 13.6 %all_to_all.50.spread_ref = bf16[16,2,4096]{2,1,0:T(2,128)(2,1)S(1)} all-to-all(bf16[16,2,4096]{2,1,0:T(2,128)(2,1)} %turn_product.4), channel_id=1, replica_groups={{16,17,18,19,20,21,22,23,24,25,26,27,28,29,30,31},{0,1,2,3,4,5,6,7,8,9,..., dimensions={0} | all-to-all | bytes 524288 | tf_op jit(solution)/shard_map/all_to_all | solution.py:510
  212.7 0.2 fold.6
  212.9 12.8 %all_to_all.51.gathered_ref = bf16[8,2,8192]{2,1,0:T(2,128)(2,1)} all-to-all(bf16[8,2,8192]{2,1,0:T(2,128)(2,1)S(1)} %get-tuple-element.26), channel_id=1, replica_groups=mesh['layer'=4,'row'=8] {'row'}, dimensions={0} | all-to-all | bytes 524288 | tf_op jit(solution)/shard_map/all_to_all | solution.py:516
  225.7 25.7 %turn_product.5 = bf16[8,2,4096]{2,1,0:T(2,128)(2,1)} custom-call(s32[2]{0:T(128)} %copy-done.1, bf16[8,2,8192]{2,1,0:T(2,128)(2,1)} %all_to_all.51.gathered_ref, bf16[4096,8192]{1,0:T(8,128)(2,1)} %bitcast.5.weight_ref, bf16[256,8192]{1,0:T(8,128)(2,1)} %all-gather.2.cloned.1.call-done.panel_ref, bf16[512,4096]{1,0:T(8,128)(2,1)} %get-tuple-element.21.aux_ref, ...), custom_call_target="tpu_custom_call" | custom-call | flops 1073741824 | bytes 65011712 | tf_op jit(solution)/shard_map/turn_product/pallas_call | solution.py:423
  251.3 3.4 %all-to-all-start.8 = ((bf16[8,2,4096]{2,1,0:T(2,128)(2,1)}), bf16[8,2,4096]{2,1,0:T(2,128)(2,1)S(1)}, u32[]{:S(2)}, u32[]{:S(2)}) async-start(bf16[8,2,4096]{2,1,0:T(2,128)(2,1)} %turn_product.5), calls=%async_computation.8 | async-start | bytes 262144 | tf_op jit(solution)/shard_map/all_to_all | solution.py:502
  254.8 6.7 %all-to-all-done.8.spread_ref = bf16[8,2,4096]{2,1,0:T(2,128)(2,1)S(1)} async-done(((bf16[8,2,4096]{2,1,0:T(2,128)(2,1)}), bf16[8,2,4096]{2,1,0:T(2,128)(2,1)S(1)}, u32[]{:S(2)}, u32[]{:S(2)}) %all-to-all-start.8) | async-done | bytes 131104 | tf_op jit(solution)/shard_map/all_to_all | solution.py:502
  261.4 0.9 fold.7
  262.3 0.7 fusion.4
  (17 shorter events, 0.2 us)
Async XLA Ops:
  7.2 105.7 %all-gather.2.cloned.1.call-start = ((), (), s32[]{:S(2)}) async-start(), calls=%async_computation.9 | async-start | bytes 4718592 | tf_op jit(solution)/shard_map/all_gather | solution.py:469
  8.5 19.6 %copy-start.2 = (bf16[256,1024]{1,0:T(8,128)(2,1)}, bf16[256,1024]{1,0:T(8,128)(2,1)S(1)}, u32[]{:S(2)}) copy-start(bf16[256,1024]{1,0:T(8,128)(2,1)S(1)} %convert_bitcast_fusion) | copy-start | bytes 1572868
  30.4 25.5 %all-to-all-start.1 = ((bf16[8,64,256]{2,1,0:T(8,128)(2,1)}), bf16[8,64,256]{2,1,0:T(8,128)(2,1)S(1)}, u32[]{:S(2)}, u32[]{:S(2)}) async-start(bf16[8,64,256]{2,1,0:T(8,128)(2,1)} %broadcast_in_dim.35), calls=%async_computation.1 | async-start | bytes 524288 | tf_op jit(solution)/shard_map/all_to_all | solution.py:22
  33.9 46.5 %copy-start.1 = (s32[2]{0:T(128)}, s32[2]{0:T(128)S(1)}, u32[]{:S(2)}) copy-start(s32[2]{0:T(128)S(1)} %pad_add_fusion.where_ref) | copy-start | bytes 28
  80.4 2.2 copy-start
  251.3 10.1 %all-to-all-start.8 = ((bf16[8,2,4096]{2,1,0:T(2,128)(2,1)}), bf16[8,2,4096]{2,1,0:T(2,128)(2,1)S(1)}, u32[]{:S(2)}, u32[]{:S(2)}) async-start(bf16[8,2,4096]{2,1,0:T(2,128)(2,1)} %turn_product.5), calls=%async_computation.8 | async-start | bytes 262144 | tf_op jit(solution)/shard_map/all_to_all | solution.py:502
Sparse Core Ops, SparseCore 0:
  28.3 50.8 all-gather.1
